TPU v7x, 256 devices: a whole 4x4x8 slice. The times are simulated.
256 devices in a mesh: lat: 32 (over z_lo, y, core), lev: 8 (over x, z_hi).
Axes of the slice: x: 4, y: 4, z: 8 (z_hi: 2, z_lo: 4; z = z_hi * 4 + z_lo), core: 2. Of those that a mesh axis runs over, the one named last changes fastest.
Arguments:
- u_wind: bfloat16 [128, 64, 2880], P('lat', 'lev'), may hold values from -4 to 4
- v_wind: bfloat16 [128, 64, 2880], P('lat', 'lev'), may hold values from -4 to 4
- thickness: float32 [128, 64, 2880], P('lat', 'lev'), may hold values from 0.5 to 2
- tracer: float32 [128, 64, 2880], P('lat', 'lev'), may hold values from -5 to 5
- remap_index: int32 [65], replicated, may hold values from 0 to 63, as said below
- remap_frac: float32 [65], replicated, may hold values from 0 to 1, as said below
Outputs:
- u_filtered: bfloat16 [128, 64, 2880], P('lat', 'lev')
- v_filtered: bfloat16 [128, 64, 2880], P('lat', 'lev')
- thickness_out: float32 [128, 64, 2880], P('lat', None, 'lev')
- tracer_out: float32 [128, 64, 2880], P('lat', None, 'lev')
Inputs may be any that keep to these rules, and one draw needn't show every extreme that they name: remap_index[k] is k or k - 1 for 0 < k < 64; remap_index[0] = 0 and remap_index[64] = 63. remap_frac[k] lies in [0, 0.35) where remap_index[k] = k and in (0.65, 1] where remap_index[k] = k - 1; remap_frac[0] = 0 and remap_frac[64] = 1.
All inputs are finite; a program needn't handle non-finite values.
Results may differ from a plain program's by a relative error of at most 0.0028.
Values may be sent and summed in bfloat16 or wider, within the bound.
No kernel may reach another device: no remote copies, remote signals or barrier semaphores. Data moves between devices by JAX's collectives and lax.ppermute only.
A program may use at most 64 MiB of HBM per device.

v0:
```python
import math

import jax
import jax.numpy as jnp
from jax import lax
from jax.sharding import PartitionSpec as P

COS_EDGE = math.cos(66.0 * math.pi / 180.0)


def with_halo(block, sides, width):
    for axis, dim in sides:
        count = lax.axis_size(axis)
        forward = [(i, i + 1) for i in range(count - 1)]
        backward = [(target, source) for source, target in forward]
        low = lax.ppermute(
            lax.slice_in_dim(block, block.shape[dim] - width, None, axis=dim), axis, forward
        )
        high = lax.ppermute(lax.slice_in_dim(block, 0, width, axis=dim), axis, backward)
        block = jnp.concatenate([low, block, high], axis=dim)
    return block


def hartley_table(lon_count):
    block_size = 240
    columns = jnp.arange(lon_count, dtype=jnp.int32)

    def row_block(first_row):
        row_ids = first_row + jnp.arange(block_size, dtype=jnp.int32)
        phase_index = row_ids[:, None] * columns[None, :] % lon_count
        angles = 2.0 * jnp.pi / lon_count * phase_index.astype(jnp.float32)
        return (jnp.cos(angles) + jnp.sin(angles)).astype(jnp.bfloat16)

    starts = jnp.arange(lon_count // block_size, dtype=jnp.int32) * block_size
    return lax.map(row_block, starts).reshape(lon_count, lon_count)


def latitude_damping(lat_ids, lat_count, lon_count):
    pole_distance = jnp.minimum(lat_ids, lat_count - 1 - lat_ids)
    is_polar = 15 * pole_distance < 2 * (lat_count - 1)
    colatitude = jnp.sin(jnp.pi * pole_distance.astype(jnp.float32) / (lat_count - 1))
    damp_ratio = (colatitude / COS_EDGE) ** 2
    wavenumber = jnp.arange(lon_count, dtype=jnp.int32)
    wave_index = jnp.minimum(wavenumber, lon_count - wavenumber)
    sine_square = jnp.sin(jnp.pi * wave_index.astype(jnp.float32) / lon_count) ** 2
    sine_square = jnp.where(wave_index == 0, 1.0, sine_square)
    damping = jnp.minimum(1.0, damp_ratio[:, None] / sine_square[None, :])
    damping = jnp.where(wave_index[None, :] == 0, 1.0, damping)
    return (is_polar, damping)


def filter_block(row_block, first_lat, hartley, lat_count):
    lat_total = row_block.shape[1]
    lon_count = row_block.shape[3]
    lat_ids = first_lat + jnp.arange(lat_total, dtype=jnp.int32)
    is_polar, damping = latitude_damping(lat_ids, lat_count, lon_count)

    def transform(values):
        spectra = jnp.dot(
            values.reshape(-1, lon_count), hartley, preferred_element_type=jnp.float32
        )
        spectra = (spectra.reshape(values.shape) * damping[None, :, None, :]).astype(jnp.bfloat16)
        smooth = (
            jnp.dot(spectra.reshape(-1, lon_count), hartley, preferred_element_type=jnp.float32)
            / lon_count
        )
        smooth = smooth.reshape(values.shape)
        return jnp.where(is_polar[None, :, None, None], smooth, values.astype(jnp.float32)).astype(
            jnp.bfloat16
        )

    def unchanged(values):
        return values

    return lax.cond(jnp.any(is_polar), transform, unchanged, row_block)


def advect(field, padded, faces_x, faces_y):
    flux_x = (
        jnp.maximum(faces_x, 0.0) * jnp.roll(field, 1, axis=2) + jnp.minimum(faces_x, 0.0) * field
    )
    flux_y = jnp.maximum(faces_y, 0.0) * padded[:-1] + jnp.minimum(faces_y, 0.0) * padded[1:]
    return field - (jnp.roll(flux_x, -1, axis=2) - flux_x) - (flux_y[1:] - flux_y[:-1])


def remap_weights(remap_index, remap_frac, level_count):
    level_ids = jnp.arange(level_count, dtype=jnp.int32)
    below = (level_ids[None, :] < remap_index[:, None]).astype(jnp.float32)
    inside = (level_ids[None, :] == remap_index[:, None]).astype(jnp.float32)
    interface = below + remap_frac[:, None] * inside
    return interface[1:] - interface[:-1]


def per_device(u_wind, v_wind, thickness, tracer, remap_index, remap_frac):
    lat_rows, level_rows, lon_count = u_wind.shape
    lat_devices = lax.axis_size("lat")
    lat_count = lat_rows * lat_devices
    level_count = level_rows * lax.axis_size("lev")
    my_place = lax.axis_index("lat")
    hartley = hartley_table(lon_count)
    winds = jnp.stack([u_wind, v_wind])
    half_rows = lat_rows // 2
    upper_rows = winds[:, :half_rows]
    lower_rows = winds[:, half_rows:]
    upper_done = filter_block(upper_rows, my_place * lat_rows, hartley, lat_count)
    lower_done = filter_block(lower_rows, my_place * lat_rows + half_rows, hartley, lat_count)
    filtered = jnp.concatenate([upper_done, lower_done], axis=1)
    courant = jnp.clip(0.05 * filtered.astype(jnp.float32), -0.15, 0.15)
    courant_x = courant[0]
    mass = tracer * thickness
    stacked = jnp.stack([thickness, mass, courant[1]])
    extended = with_halo(stacked.astype(jnp.bfloat16), (("lat", 1),), 1).astype(stacked.dtype)
    courant_ext = extended[2]
    faces_y = 0.5 * (courant_ext[:-1] + courant_ext[1:])
    face_ids = my_place * lat_rows + jnp.arange(lat_rows + 1, dtype=jnp.int32)
    at_pole = jnp.logical_or(face_ids == 0, face_ids == lat_count)
    faces_y = jnp.where(at_pole[:, None, None], 0.0, faces_y)
    faces_x = 0.5 * (jnp.roll(courant_x, 1, axis=2) + courant_x)
    thick_adv = advect(thickness, extended[0], faces_x, faces_y)
    mass_adv = advect(mass, extended[1], faces_x, faces_y)
    weights = remap_weights(remap_index, remap_frac, level_count)
    thick_cols = lax.all_to_all(thick_adv, "lev", split_axis=2, concat_axis=1, tiled=True)
    mass_cols = lax.all_to_all(mass_adv, "lev", split_axis=2, concat_axis=1, tiled=True)
    new_thick = jnp.einsum("kl,jlx->jkx", weights, thick_cols, precision=lax.Precision.HIGHEST)
    new_mass = jnp.einsum("kl,jlx->jkx", weights, mass_cols, precision=lax.Precision.HIGHEST)
    tracer_out = new_mass / new_thick
    return (filtered[0], filtered[1], new_thick, tracer_out)


def solution(mesh):
    placed = (
        P("lat", "lev", None),
        P("lat", "lev", None),
        P("lat", "lev", None),
        P("lat", "lev", None),
        P(),
        P(),
    )
    return jax.shard_map(
        per_device,
        mesh=mesh,
        in_specs=placed,
        out_specs=(
            P("lat", "lev", None),
            P("lat", "lev", None),
            P("lat", None, "lev"),
            P("lat", None, "lev"),
        ),
        check_vma=False,
    )
```

profile of v0, /device:TPU:1, one launch (start us, length us, event | category | flops | bytes accessed | tf_op | source)
XLA Modules:
  0.0 305.4 jit_solution(1010886022819398528)
XLA Ops:
  1.4 182.9 %while.13 = (s32[]{:T(128)}, bf16[12,240,2880]{2,1,0:T(8,128)(2,1)}, s32[12]{0:T(128)S(1)}, s32[]{:T(128)}) while((s32[]{:T(128)}, bf16[12,240,2880]{2,1,0:T(8,128)(2,1)}, s32[12]{0:T(128)S(1)}, s32[]{:T(128)}) %tuple.60), condition=%wide.region_2.3_spmd.clone, body=%wide.region_1.2_spmd.clone.sunk | while | flops 7603442 | bytes 1415621 | solution.py:35
  2.7 14.0 %fusion.72 = bf16[12,240,2880]{2,1,0:T(8,128)(2,1)} fusion(bf16[12,240,2880]{2,1,0:T(8,128)(2,1)} %get-tuple-element.236, s32[]{:T(128)} %get-tuple-element.235, s32[240]{0:T(256)S(1)} %iota_add_fusion.2), kind=kLoop, calls=%fused_computation.29.clone.1 | loop fusion | flops 7603200 | bytes 1414592 | tf_op jit(solution)/shard_map/while/body/jit(dynamic_update_index_in_dim)/dynamic_update_slice | solution.py:35
  17.9 14.0 %fusion.72 = bf16[12,240,2880]{2,1,0:T(8,128)(2,1)} fusion(bf16[12,240,2880]{2,1,0:T(8,128)(2,1)} %get-tuple-element.236, s32[]{:T(128)} %get-tuple-element.235, s32[240]{0:T(256)S(1)} %iota_add_fusion.2), kind=kLoop, calls=%fused_computation.29.clone.1 | loop fusion | flops 7603200 | bytes 1414592 | tf_op jit(solution)/shard_map/while/body/jit(dynamic_update_index_in_dim)/dynamic_update_slice | solution.py:35
  33.2 14.0 %fusion.72 = bf16[12,240,2880]{2,1,0:T(8,128)(2,1)} fusion(bf16[12,240,2880]{2,1,0:T(8,128)(2,1)} %get-tuple-element.236, s32[]{:T(128)} %get-tuple-element.235, s32[240]{0:T(256)S(1)} %iota_add_fusion.2), kind=kLoop, calls=%fused_computation.29.clone.1 | loop fusion | flops 7603200 | bytes 1414592 | tf_op jit(solution)/shard_map/while/body/jit(dynamic_update_index_in_dim)/dynamic_update_slice | solution.py:35
  48.4 14.0 %fusion.72 = bf16[12,240,2880]{2,1,0:T(8,128)(2,1)} fusion(bf16[12,240,2880]{2,1,0:T(8,128)(2,1)} %get-tuple-element.236, s32[]{:T(128)} %get-tuple-element.235, s32[240]{0:T(256)S(1)} %iota_add_fusion.2), kind=kLoop, calls=%fused_computation.29.clone.1 | loop fusion | flops 7603200 | bytes 1414592 | tf_op jit(solution)/shard_map/while/body/jit(dynamic_update_index_in_dim)/dynamic_update_slice | solution.py:35
  63.7 14.0 %fusion.72 = bf16[12,240,2880]{2,1,0:T(8,128)(2,1)} fusion(bf16[12,240,2880]{2,1,0:T(8,128)(2,1)} %get-tuple-element.236, s32[]{:T(128)} %get-tuple-element.235, s32[240]{0:T(256)S(1)} %iota_add_fusion.2), kind=kLoop, calls=%fused_computation.29.clone.1 | loop fusion | flops 7603200 | bytes 1414592 | tf_op jit(solution)/shard_map/while/body/jit(dynamic_update_index_in_dim)/dynamic_update_slice | solution.py:35
  78.9 14.0 %fusion.72 = bf16[12,240,2880]{2,1,0:T(8,128)(2,1)} fusion(bf16[12,240,2880]{2,1,0:T(8,128)(2,1)} %get-tuple-element.236, s32[]{:T(128)} %get-tuple-element.235, s32[240]{0:T(256)S(1)} %iota_add_fusion.2), kind=kLoop, calls=%fused_computation.29.clone.1 | loop fusion | flops 7603200 | bytes 1414592 | tf_op jit(solution)/shard_map/while/body/jit(dynamic_update_index_in_dim)/dynamic_update_slice | solution.py:35
  94.2 14.0 %fusion.72 = bf16[12,240,2880]{2,1,0:T(8,128)(2,1)} fusion(bf16[12,240,2880]{2,1,0:T(8,128)(2,1)} %get-tuple-element.236, s32[]{:T(128)} %get-tuple-element.235, s32[240]{0:T(256)S(1)} %iota_add_fusion.2), kind=kLoop, calls=%fused_computation.29.clone.1 | loop fusion | flops 7603200 | bytes 1414592 | tf_op jit(solution)/shard_map/while/body/jit(dynamic_update_index_in_dim)/dynamic_update_slice | solution.py:35
  109.4 14.0 %fusion.72 = bf16[12,240,2880]{2,1,0:T(8,128)(2,1)} fusion(bf16[12,240,2880]{2,1,0:T(8,128)(2,1)} %get-tuple-element.236, s32[]{:T(128)} %get-tuple-element.235, s32[240]{0:T(256)S(1)} %iota_add_fusion.2), kind=kLoop, calls=%fused_computation.29.clone.1 | loop fusion | flops 7603200 | bytes 1414592 | tf_op jit(solution)/shard_map/while/body/jit(dynamic_update_index_in_dim)/dynamic_update_slice | solution.py:35
  124.6 14.0 %fusion.72 = bf16[12,240,2880]{2,1,0:T(8,128)(2,1)} fusion(bf16[12,240,2880]{2,1,0:T(8,128)(2,1)} %get-tuple-element.236, s32[]{:T(128)} %get-tuple-element.235, s32[240]{0:T(256)S(1)} %iota_add_fusion.2), kind=kLoop, calls=%fused_computation.29.clone.1 | loop fusion | flops 7603200 | bytes 1414592 | tf_op jit(solution)/shard_map/while/body/jit(dynamic_update_index_in_dim)/dynamic_update_slice | solution.py:35
  139.9 14.0 %fusion.72 = bf16[12,240,2880]{2,1,0:T(8,128)(2,1)} fusion(bf16[12,240,2880]{2,1,0:T(8,128)(2,1)} %get-tuple-element.236, s32[]{:T(128)} %get-tuple-element.235, s32[240]{0:T(256)S(1)} %iota_add_fusion.2), kind=kLoop, calls=%fused_computation.29.clone.1 | loop fusion | flops 7603200 | bytes 1414592 | tf_op jit(solution)/shard_map/while/body/jit(dynamic_update_index_in_dim)/dynamic_update_slice | solution.py:35
  155.1 14.0 %fusion.72 = bf16[12,240,2880]{2,1,0:T(8,128)(2,1)} fusion(bf16[12,240,2880]{2,1,0:T(8,128)(2,1)} %get-tuple-element.236, s32[]{:T(128)} %get-tuple-element.235, s32[240]{0:T(256)S(1)} %iota_add_fusion.2), kind=kLoop, calls=%fused_computation.29.clone.1 | loop fusion | flops 7603200 | bytes 1414592 | tf_op jit(solution)/shard_map/while/body/jit(dynamic_update_index_in_dim)/dynamic_update_slice | solution.py:35
  170.4 14.0 %fusion.72 = bf16[12,240,2880]{2,1,0:T(8,128)(2,1)} fusion(bf16[12,240,2880]{2,1,0:T(8,128)(2,1)} %get-tuple-element.236, s32[]{:T(128)} %get-tuple-element.235, s32[240]{0:T(256)S(1)} %iota_add_fusion.2), kind=kLoop, calls=%fused_computation.29.clone.1 | loop fusion | flops 7603200 | bytes 1414592 | tf_op jit(solution)/shard_map/while/body/jit(dynamic_update_index_in_dim)/dynamic_update_slice | solution.py:35
  185.8 13.4 %conditional.3 = (bf16[2,2,8,2880]{3,2,1,0:T(8,128)(2,1)S(1)}) conditional(s32[]{:T(128)} %convert_element_type.100, bf16[2,2,8,2880]{3,2,1,0:T(8,128)(2,1)S(1)} %get-tuple-element.208, (pred[2]{0:T(512)(128)(4,1)S(1)}, bf16[2,2,8,2880]{3,2,1,0:T(8,128)(2,1)S(1)}, bf16[2880,2880]{1,0:T(8,128)(2,1)}, pred[2880]{0:T(1024)(128)(4,1)S(1)}, ...), branch_computations={%region_6.7_spmd, %region_7.8_spmd} | conditional | flops 1062253440 | bytes 100918152 | solution.py:75
  185.9 8.3 %fusion.15 = bf16[2,2,8,2880]{3,2,1,0:T(8,128)(2,1)S(1)} fusion(bf16[2,2,8,2880]{3,2,1,0:T(8,128)(2,1)S(1)} %get-tuple-element.166, bf16[2880,2880]{1,0:T(8,128)(2,1)} %get-tuple-element.167, f32[2,2880]{1,0:T(2,128)S(1)} %minimum_select_fusion.1), kind=kOutput, calls=%fused_computation.13 | convolution fusion | flops 531025920 | bytes 16980480 | tf_op jit(solution)/shard_map/cond/branch_1_fun/dot_general | solution.py:59
  199.2 13.4 %conditional.2 = (bf16[2,2,8,2880]{3,2,1,0:T(8,128)(2,1)S(1)}) conditional(s32[]{:T(128)} %convert_element_type.97, bf16[2,2,8,2880]{3,2,1,0:T(8,128)(2,1)S(1)} %get-tuple-element.209, (pred[2]{0:T(512)(128)(4,1)S(1)}, bf16[2,2,8,2880]{3,2,1,0:T(8,128)(2,1)S(1)}, bf16[2880,2880]{1,0:T(8,128)(2,1)}, pred[2880]{0:T(1024)(128)(4,1)S(1)}, ...), branch_computations={%region_3.4_spmd, %region_4.5_spmd} | conditional | flops 1062253440 | bytes 100918152 | solution.py:75
  199.4 8.3 %fusion.7 = bf16[2,2,8,2880]{3,2,1,0:T(8,128)(2,1)S(1)} fusion(bf16[2,2,8,2880]{3,2,1,0:T(8,128)(2,1)S(1)} %get-tuple-element.158, bf16[2880,2880]{1,0:T(8,128)(2,1)} %get-tuple-element.159, f32[2,2880]{1,0:T(2,128)S(1)} %minimum_select_fusion), kind=kOutput, calls=%fused_computation.5 | convolution fusion | flops 531025920 | bytes 16980480 | tf_op jit(solution)/shard_map/cond/branch_1_fun/dot_general | solution.py:59
  213.5 4.6 %collective-permute-start = (bf16[3,1,8,2880]{3,2,1,0:T(8,128)(2,1)S(1)}, bf16[3,1,8,2880]{3,2,1,0:T(8,128)(2,1)S(1)}, u32[]{:S(2)}, u32[]{:S(2)}) collective-permute-start(bf16[3,1,8,2880]{3,2,1,0:T(8,128)(2,1)S(1)} %get-tuple-element.203), channel_id=1, source_target_pairs={{0,8},{8,16},{16,24},{24,32},{32,40},{40,48},{48,56},{56,64},{64,7... | collective-permute-start | bytes 414728 | tf_op jit(solution)/shard_map/ppermute | solution.py:16
  229.4 9.0 %reshape.195 = f32[8,1,11520]{2,1,0:T(1,128)} reshape(f32[2880,4,8]{2,1,0:T(4,128)} %bitcast.115) | data formatting | bytes 737280
  238.4 10.6 %all-to-all-start.1 = ((f32[8,1,11520]{2,1,0:T(1,128)}), f32[8,1,11520]{2,1,0:T(1,128)S(1)}, u32[]{:S(2)}, u32[]{:S(2)}) async-start(f32[8,1,11520]{2,1,0:T(1,128)} %reshape.195), calls=%async_computation.1 | async-start | bytes 737280 | tf_op jit(solution)/shard_map/all_to_all | solution.py:123
  253.5 9.0 %reshape.193 = f32[8,1,11520]{2,1,0:T(1,128)} reshape(f32[2880,4,8]{2,1,0:T(4,128)} %bitcast.116) | data formatting | bytes 737280
  262.5 9.1 %all-to-all-start = ((f32[8,1,11520]{2,1,0:T(1,128)}), f32[8,1,11520]{2,1,0:T(1,128)S(1)}, u32[]{:S(2)}, u32[]{:S(2)}) async-start(f32[8,1,11520]{2,1,0:T(1,128)} %reshape.193), calls=%async_computation | async-start | bytes 737280 | tf_op jit(solution)/shard_map/all_to_all | solution.py:122
  274.5 9.6 %reshape.196 = f32[2880,4,8]{2,1,0:T(4,128)} reshape(f32[8,11520]{1,0:T(8,128)S(1)} %reduce.1) | data formatting | bytes 737280
  289.8 9.6 %reshape.194 = f32[2880,4,8]{2,1,0:T(4,128)} reshape(f32[8,11520]{1,0:T(8,128)S(1)} %reduce) | data formatting | bytes 737280
  (97 shorter events, 56.7 us)
Async XLA Ops:
  1.4 184.2 %copy-start.5 = (bf16[4,8,2880]{2,1,0:T(8,128)(2,1)S(1)}, bf16[4,8,2880]{2,1,0:T(8,128)(2,1)}, u32[]{:S(2)}) copy-start(bf16[4,8,2880]{2,1,0:T(8,128)(2,1)} %param.13) | copy-start | bytes 552964
  1.4 184.2 %copy-start.6 = (bf16[4,8,2880]{2,1,0:T(8,128)(2,1)S(1)}, bf16[4,8,2880]{2,1,0:T(8,128)(2,1)}, u32[]{:S(2)}) copy-start(bf16[4,8,2880]{2,1,0:T(8,128)(2,1)} %param.12) | copy-start | bytes 552964
  185.9 10.6 %copy-start = (bf16[2880,2880]{1,0:T(8,128)(2,1)S(1)}, bf16[2880,2880]{1,0:T(8,128)(2,1)}, u32[]{:S(2)}) copy-start(bf16[2880,2880]{1,0:T(8,128)(2,1)} %get-tuple-element.167) | copy-start | bytes 49766404 | tf_op jit(solution)/shard_map/cond
  199.2 13.7 %copy-start.2 = (f32[4,8,2880]{2,1,0:T(8,128)S(1)}, f32[4,8,2880]{2,1,0:T(8,128)}, u32[]{:S(2)}) copy-start(f32[4,8,2880]{2,1,0:T(8,128)} %param.14) | copy-start | bytes 1105924
  199.2 13.8 %copy-start.4 = (f32[4,8,2880]{2,1,0:T(8,128)S(1)}, f32[4,8,2880]{2,1,0:T(8,128)}, u32[]{:S(2)}) copy-start(f32[4,8,2880]{2,1,0:T(8,128)} %param.15) | copy-start | bytes 1105924
  199.3 10.7 %copy-start.1 = (bf16[2880,2880]{1,0:T(8,128)(2,1)S(1)}, bf16[2880,2880]{1,0:T(8,128)(2,1)}, u32[]{:S(2)}) copy-start(bf16[2880,2880]{1,0:T(8,128)(2,1)} %get-tuple-element.159) | copy-start | bytes 49766404 | tf_op jit(solution)/shard_map/cond
  213.5 7.1 %collective-permute-start = (bf16[3,1,8,2880]{3,2,1,0:T(8,128)(2,1)S(1)}, bf16[3,1,8,2880]{3,2,1,0:T(8,128)(2,1)S(1)}, u32[]{:S(2)}, u32[]{:S(2)}) collective-permute-start(bf16[3,1,8,2880]{3,2,1,0:T(8,128)(2,1)S(1)} %get-tuple-element.203), channel_id=1, source_target_pairs={{0,8},{8,16},{16,24},{24,32},{32,40},{40,48},{48,56},{56,64},{64,7... | collective-permute-start | bytes 414728 | tf_op jit(solution)/shard_map/ppermute | solution.py:16
  218.1 6.4 %collective-permute-start.1 = (bf16[3,1,8,2880]{3,2,1,0:T(8,128)(2,1)S(1)}, bf16[3,1,8,2880]{3,2,1,0:T(8,128)(2,1)S(1)}, u32[]{:S(2)}, u32[]{:S(2)}) collective-permute-start(bf16[3,1,8,2880]{3,2,1,0:T(8,128)(2,1)S(1)} %get-tuple-element.204), channel_id=1, source_target_pairs={{8,0},{16,8},{24,16},{32,24},{40,32},{48,40},{56,48},{64,56},{72,6... | collective-permute-start | bytes 414728 | tf_op jit(solution)/shard_map/ppermute | solution.py:19
  238.4 24.1 %all-to-all-start.1 = ((f32[8,1,11520]{2,1,0:T(1,128)}), f32[8,1,11520]{2,1,0:T(1,128)S(1)}, u32[]{:S(2)}, u32[]{:S(2)}) async-start(f32[8,1,11520]{2,1,0:T(1,128)} %reshape.195), calls=%async_computation.1 | async-start | bytes 737280 | tf_op jit(solution)/shard_map/all_to_all | solution.py:123
  249.1 22.5 %copy-start.7 = (f32[65]{0:T(128)S(1)}, f32[65]{0:T(128)}, u32[]{:S(2)}) copy-start(f32[65]{0:T(128)} %param.17) | copy-start | bytes 784
  249.2 22.4 %copy-start.8 = (s32[65]{0:T(128)S(1)}, s32[65]{0:T(128)}, u32[]{:S(2)}) copy-start(s32[65]{0:T(128)} %param.16) | copy-start | bytes 784
  262.5 25.7 %all-to-all-start = ((f32[8,1,11520]{2,1,0:T(1,128)}), f32[8,1,11520]{2,1,0:T(1,128)S(1)}, u32[]{:S(2)}, u32[]{:S(2)}) async-start(f32[8,1,11520]{2,1,0:T(1,128)} %reshape.193), calls=%async_computation | async-start | bytes 737280 | tf_op jit(solution)/shard_map/all_to_all | solution.py:122
  304.1 1.3 copy-start.3
where the time goes:
time: 306 us; the launch traced here: 305 us
  other arithmetic  182 us (59%)
  local copies, waits for them, and re-layouts  67 us (22%)
  starting transfers between devices  26.4 us (9%)
  matrix products  23.4 us (8%)
  waiting for transfers between devices  3.93 us (1%)
    dynamic_update_slice x12, other arithmetic, hartley_table(): return lax.map(row_block, starts).reshape(lon_count, lon_count)  168 us
    unnamed x18, local copies, waits for them, and re-layouts  37.2 us
    dot_general x2, matrix products, transform(): jnp.dot(values.reshape(-1, lon_count), hartley, preferred_element_type=jn...  16.7 us
    all_to_all x1, starting transfers between devices, per_device(): lax.all_to_all(mass_adv, 'lev', split_axis=2, concat_axis=1, tiled=True)  10.6 us
    all_to_all x1, starting transfers between devices, per_device(): lax.all_to_all(thick_adv, 'lev', split_axis=2, concat_axis=1, tiled=True)  9.05 us
    sub x2, local copies, waits for them, and re-layouts, advect(): field - (jnp.roll(flux_x, -1, axis=2) - flux_x) - (flux_y[1:] - flux_y[:-1])  8.71 us
    add x12, other arithmetic, row_block(): row_ids = first_row + jnp.arange(block_size, dtype=jnp.int32)  7.76 us
    dynamic_slice x12, local copies, waits for them, and re-layouts, hartley_table(): return lax.map(row_block, starts).reshape(lon_count, lon_count)  6.99 us
  transfers between devices with their start and end apart: 4, of which 1 were waited for; matrix products, arithmetic and copies ran while one was open for 10% of the time, Pallas kernels for 0%

commit v1 on v0

v1 whole, which is shorter than its diff:
```python
import functools
import math

import jax
import jax.numpy as jnp
import ml_dtypes
import numpy as np
from jax import lax
from jax.experimental import pallas as pl
from jax.experimental.pallas import tpu as pltpu
from jax.sharding import PartitionSpec as P

COS_EDGE = math.cos(66.0 * math.pi / 180.0)
LANES = 128
THICK_MID = 1.25


def padded_to(count):
    return -(-count // LANES) * LANES


def filter_parts(lon_count):
    parts = []
    column = 0
    for first, step, points in (
        (1, 2, lon_count // 2),
        (2, 4, lon_count // 4),
        (4, 8, lon_count // 8),
        (0, 8, lon_count // 8),
    ):
        parts.append((first, step, points, column))
        column += padded_to(points)
    return parts, column


def table_places(parts):
    odd, two, four, eight = (padded_to(part[2]) for part in parts)
    return [(0, 0, odd), (0, odd, two), (two, odd, four), (two, odd + four, eight)]


def filter_tables(lat_count, lon_count):
    phase = 2.0 * np.pi * np.arange(lon_count) / lon_count
    rounded = (np.cos(phase) + np.sin(phase)).astype(np.float32).astype(ml_dtypes.bfloat16)
    polar = [d for d in range((lat_count + 1) // 2) if 15 * d < 2 * (lat_count - 1)]
    ratio = (np.sin(np.pi * np.array(polar, np.float64) / (lat_count - 1)) / COS_EDGE) ** 2
    wave = np.arange(lon_count)
    wave = np.minimum(wave, lon_count - wave)
    sine_square = np.sin(np.pi * wave / lon_count) ** 2
    sine_square[0] = 1.0
    values = np.minimum(1.0, ratio[:, None] / sine_square[None, :])
    values[:, 0] = 1.0

    parts, columns = filter_parts(lon_count)
    places = table_places(parts)
    tables = np.zeros((places[0][2], places[0][2] + places[1][2]), ml_dtypes.bfloat16)
    damping = np.zeros((len(polar), 1, columns), np.float32)
    for (first, step, points, column), (row, left, _) in zip(parts, places):
        waves = first + step * np.arange(points)
        tables[row : row + points, left : left + points] = rounded[
            np.arange(points)[:, None] * waves[None, :] % lon_count
        ]
        damping[:, 0, column : column + points] = values[:, waves]
    return tables, damping


def filter_advect(
    lat_count,
    u_ref,
    v_ref,
    thick_ref,
    tracer_ref,
    low_ref,
    high_ref,
    table_ref,
    damp_ref,
    u_out,
    v_out,
    send_ref,
    real_ref,
    work_ref,
    split_ref,
    prod_ref,
    spec_ref,
    edge_ref,
):
    lat_rows, level_rows, lon_count = u_ref.shape
    sectors = send_ref.shape[0]
    sector_wide = send_ref.shape[2]
    sector = lon_count // sectors
    groups, _, padded = real_ref.shape
    distances = damp_ref.shape[0]
    first_lat = lax.axis_index("lat") * lat_rows
    f32 = jnp.float32
    bf16 = jnp.bfloat16
    parts, columns = filter_parts(lon_count)
    places = table_places(parts)

    def distance(lat):
        return jnp.minimum(lat, lat_count - 1 - lat)

    def is_polar(lat):
        return jnp.logical_and(distance(lat) >= 0, 15 * distance(lat) < 2 * (lat_count - 1))

    edge_ref[0] = low_ref[0].astype(f32)
    edge_ref[1] = high_ref[0].astype(f32)
    u_out[...] = u_ref[...]
    v_out[...] = v_ref[...]

    needs_filter = is_polar(first_lat)
    for offset in (-1, lat_rows - 1, lat_rows):
        needs_filter = jnp.logical_or(needs_filter, is_polar(first_lat + offset))

    @pl.when(needs_filter)
    def _():
        half, quarter, eighth = parts[0][2], parts[1][2], parts[2][2]
        half_wide, quarter_wide, eighth_wide = (padded_to(part[2]) for part in parts[:3])
        lats = [first_lat + j for j in range(lat_rows)]
        lats = lats + lats + [first_lat - 1, first_lat + lat_rows]
        for g in range(groups):
            if g < lat_rows:
                wind = u_ref[g].astype(f32)
            elif g < 2 * lat_rows:
                wind = v_ref[g - lat_rows].astype(f32)
            else:
                wind = edge_ref[g - 2 * lat_rows]
            real_ref[g, :, lon_count:] = jnp.zeros((level_rows, padded - lon_count), f32)
            real_ref[g, :, :lon_count] = wind
            near = real_ref[g, :, :half_wide]
            far = real_ref[g, :, half : half + half_wide]
            odd, even = near - far, near + far
            work_ref[g, :, :half_wide] = even
            near = even[:, :quarter_wide]
            far = work_ref[g, :, quarter : quarter + quarter_wide]
            two, even = near - far, near + far
            work_ref[g, :, half_wide : half_wide + quarter_wide] = even
            near = even[:, :eighth_wide]
            far = work_ref[g, :, half_wide + eighth : half_wide + eighth + eighth_wide]
            row = jnp.concatenate([odd, two, near - far, near + far], axis=1)
            high = row.astype(bf16).astype(f32)
            both = jnp.concatenate([high, row - high], axis=0)
            split_ref[2 * level_rows * g : 2 * level_rows * (g + 1), :] = both.astype(bf16)
        for (_, _, _, column), (top, left, size) in zip(parts, places):
            prod_ref[:, column : column + size] = jnp.dot(
                split_ref[:, column : column + size],
                table_ref[top : top + size, left : left + size],
                preferred_element_type=f32,
            )
        for g in range(0, groups, 2):
            pair = []
            for member in (g, g + 1):
                start = 2 * level_rows * member
                spectra = (
                    prod_ref[start : start + level_rows, :]
                    + prod_ref[start + level_rows : start + 2 * level_rows, :]
                )
                place = jnp.clip(distance(lats[member]), 0, distances - 1)
                pair.append(spectra * damp_ref[place])
            spec_ref[level_rows * g : level_rows * (g + 2), :] = jnp.concatenate(
                pair, axis=0
            ).astype(bf16)
        rows = groups * level_rows
        for (_, _, _, column), (top, left, size) in zip(parts, places):
            prod_ref[:rows, column : column + size] = lax.dot_general(
                spec_ref[:, column : column + size],
                table_ref[top : top + size, left : left + size],
                (((1,), (1,)), ((), ())),
                preferred_element_type=f32,
            )
        for g in range(groups):
            start = level_rows * g
            odd, two, four, eight = (
                prod_ref[start : start + level_rows, column : column + padded_to(points)]
                for _, _, points, column in parts
            )
            work_ref[g, :, :eighth_wide] = eight + four
            work_ref[g, :, eighth : 2 * eighth] = (eight - four)[:, :eighth]
            even = work_ref[g, :, :quarter_wide]
            work_ref[g, :, :quarter_wide] = even + two
            work_ref[g, :, quarter : 2 * quarter] = (even - two)[:, :quarter]
            even = work_ref[g, :, :half_wide]
            scale = 1.0 / lon_count
            real_ref[g, :, :half_wide] = (even + odd) * scale
            real_ref[g, :, half : 2 * half] = ((even - odd) * scale)[:, :half]
        for g in range(2 * lat_rows):
            out = u_out if g < lat_rows else v_out

            @pl.when(is_polar(lats[g]))
            def _():
                out[g % lat_rows] = real_ref[g, :, :lon_count].astype(bf16)

        for side in range(2):

            @pl.when(is_polar(lats[2 * lat_rows + side]))
            def _():
                smooth = real_ref[2 * lat_rows + side, :, :lon_count]
                edge_ref[side] = smooth.astype(bf16).astype(f32)

    whole = lon_count // LANES * LANES
    rest = lon_count - whole
    lane = lax.broadcasted_iota(jnp.int32, (level_rows, LANES), 1)

    def courant(wind):
        return jnp.clip(0.05 * wind, -0.15, 0.15)

    def extend(ref, index, value):
        ref[index, :, :lon_count] = value
        tail = jnp.where(
            lane < rest,
            ref[index, :, whole : whole + LANES],
            pltpu.roll(ref[index, :, :LANES], rest, 1),
        )
        ends = pltpu.roll(tail, LANES - rest, 1)
        return jnp.concatenate([ref[index, :, :whole], tail, ends], axis=1)

    def before(value):
        return pltpu.roll(value, 1, 1)

    def after(value):
        return pltpu.roll(value, padded - 1, 1)

    def plain(index, value):
        real_ref[index, :, :lon_count] = value
        return real_ref[index]

    fields_below = (low_ref[1].astype(f32), low_ref[2].astype(f32))
    courant_below = courant(edge_ref[0])
    flux_below = None
    for j in range(lat_rows):
        thick = thick_ref[j]
        mass = tracer_ref[j] * thick
        courant_here = courant(v_out[j].astype(f32))
        if j == 0:
            face = 0.5 * (courant_below + courant_here)
            face = jnp.where(first_lat == 0, jnp.zeros_like(face), face)
            flux_below = [
                jnp.maximum(face, 0.0) * below + jnp.minimum(face, 0.0) * here
                for below, here in zip(fields_below, (thick, mass))
            ]
        if j == lat_rows - 1:
            courant_above = courant(edge_ref[1])
            thick_above = high_ref[1].astype(f32)
            mass_above = high_ref[2].astype(f32)
        else:
            courant_above = courant(v_out[j + 1].astype(f32))
            thick_above = thick_ref[j + 1]
            mass_above = tracer_ref[j + 1] * thick_above
        face = 0.5 * (courant_here + courant_above)
        if j == lat_rows - 1:
            at_end = first_lat + lat_rows == lat_count
            face = jnp.where(at_end, jnp.zeros_like(face), face)
        rise, fall = jnp.maximum(face, 0.0), jnp.minimum(face, 0.0)
        flux_above = [rise * thick + fall * thick_above, rise * mass + fall * mass_above]
        courant_x = extend(real_ref, 0, courant(u_out[j].astype(f32)))
        face_x = 0.5 * (before(courant_x) + courant_x)
        rise_x, fall_x = jnp.maximum(face_x, 0.0), jnp.minimum(face_x, 0.0)
        moved = []
        for index, field in enumerate((thick, mass)):
            field_x = extend(real_ref, 1 + index, field)
            flux_x = rise_x * before(field_x) + fall_x * field_x
            across = flux_above[index] - flux_below[index]
            result = field_x - (after(flux_x) - flux_x) - plain(3 + index, across)
            moved.append(result)
        moved[0] = moved[0] - THICK_MID
        both = jnp.concatenate(moved, axis=0)
        for s in range(sectors):
            block = both[:, s * sector : s * sector + sector_wide]
            send_ref[s, 2 * level_rows * j : 2 * level_rows * (j + 1), :] = block.astype(bf16)
        flux_below = flux_above


def remap(index_ref, frac_ref, recv_ref, thick_out, tracer_out):
    lat_rows, level_count, sector = thick_out.shape
    sources, _, wide = recv_ref.shape
    level_rows = level_count // sources
    f32 = jnp.float32
    lanes = index_ref.shape[1]
    target = lax.broadcasted_iota(jnp.int32, (1, lanes), 1)
    own = index_ref[...] == target
    frac = frac_ref[...]
    inner = jnp.where(own, 1.0, frac)
    outer = jnp.where(own, frac, 0.0)
    inner_next = pltpu.roll(inner, lanes - 1, 1)
    outer_next = pltpu.roll(outer, lanes - 1, 1)
    rows = lax.broadcasted_iota(jnp.int32, (level_count, lanes), 0)
    columns = lax.broadcasted_iota(jnp.int32, (level_count, lanes), 1)
    diagonal = rows == columns

    def column(row):
        spread = jnp.where(diagonal, jnp.broadcast_to(row, diagonal.shape), 0.0)
        return jnp.broadcast_to(jnp.sum(spread, axis=1, keepdims=True), (level_count, wide))

    below, here, above = column(1.0 - inner), column(inner_next - outer), column(outer_next)
    place = lax.broadcasted_iota(jnp.int32, (level_rows, wide), 0)
    top, bottom = place == 0, place == level_rows - 1
    for j in range(lat_rows):
        blocks = [
            recv_ref[source, 2 * level_rows * j : 2 * level_rows * (j + 1), :].astype(f32)
            for source in range(sources)
        ]
        results = []
        for index in range(2):
            layers = [block[level_rows * index : level_rows * (index + 1)] for block in blocks]
            if index == 0:
                layers = [layer + THICK_MID for layer in layers]
            down = [pltpu.roll(layer, 1, 0) for layer in layers]
            up = [pltpu.roll(layer, level_rows - 1, 0) for layer in layers]
            outs = []
            for source in range(sources):
                chosen = slice(level_rows * source, level_rows * (source + 1))
                lower = jnp.where(top, down[max(source - 1, 0)], down[source])
                higher = jnp.where(bottom, up[min(source + 1, sources - 1)], up[source])
                outs.append(
                    below[chosen] * lower + here[chosen] * layers[source] + above[chosen] * higher
                )
            results.append(outs)
        for source in range(sources):
            chosen = slice(level_rows * source, level_rows * (source + 1))
            thick, mass = results[0][source], results[1][source]
            thick_out[j, chosen, :] = thick[:, :sector]
            tracer_out[j, chosen, :] = (mass / thick)[:, :sector]


def per_device(u_wind, v_wind, thickness, tracer, remap_index, remap_frac):
    lat_rows, level_rows, lon_count = u_wind.shape
    lat_devices = lax.axis_size("lat")
    lat_count = lat_rows * lat_devices
    sectors = lax.axis_size("lev")
    level_count = level_rows * sectors
    sector = lon_count // sectors
    sector_wide = padded_to(sector)
    tables, damping = filter_tables(lat_count, lon_count)
    columns = damping.shape[2]
    padded = (lon_count // LANES + 2) * LANES
    f32, bf16 = jnp.float32, jnp.bfloat16

    def edge(row):
        thick = thickness[row]
        mass = tracer[row] * thick
        return jnp.stack([v_wind[row], thick.astype(bf16), mass.astype(bf16)])

    forward = [(i, i + 1) for i in range(lat_devices - 1)]
    backward = [(target, source) for source, target in forward]
    low = lax.ppermute(edge(lat_rows - 1), "lat", forward)
    high = lax.ppermute(edge(0), "lat", backward)
    groups = 2 * lat_rows + 2
    u_filtered, v_filtered, send = pl.pallas_call(
        functools.partial(filter_advect, lat_count),
        out_shape=(
            jax.ShapeDtypeStruct(u_wind.shape, bf16),
            jax.ShapeDtypeStruct(v_wind.shape, bf16),
            jax.ShapeDtypeStruct((sectors, 2 * lat_rows * level_rows, sector_wide), bf16),
        ),
        scratch_shapes=[
            pltpu.VMEM((groups, level_rows, padded), f32),
            pltpu.VMEM((groups, level_rows, padded), f32),
            pltpu.VMEM((2 * groups * level_rows, columns), bf16),
            pltpu.VMEM((2 * groups * level_rows, columns), f32),
            pltpu.VMEM((groups * level_rows, columns), bf16),
            pltpu.VMEM((2, level_rows, lon_count), f32),
        ],
        compiler_params=pltpu.CompilerParams(vmem_limit_bytes=40 * 1024 * 1024),
        name="filter_advect",
    )(u_wind, v_wind, thickness, tracer, low, high, tables, damping)
    recv = lax.all_to_all(send, "lev", split_axis=0, concat_axis=0, tiled=True)
    spare = -(level_count + 1) % LANES
    index_row = jnp.pad(remap_index, (0, spare))[None, :]
    frac_row = jnp.pad(remap_frac, (0, spare))[None, :]
    out = jax.ShapeDtypeStruct((lat_rows, level_count, sector), f32)
    thick_out, tracer_out = pl.pallas_call(
        remap,
        out_shape=(out, out),
        compiler_params=pltpu.CompilerParams(vmem_limit_bytes=32 * 1024 * 1024),
        name="remap",
    )(index_row, frac_row, recv)
    return u_filtered, v_filtered, thick_out, tracer_out


def solution(mesh):
    placed = (
        P("lat", "lev", None),
        P("lat", "lev", None),
        P("lat", "lev", None),
        P("lat", "lev", None),
        P(),
        P(),
    )
    return jax.shard_map(
        per_device,
        mesh=mesh,
        in_specs=placed,
        out_specs=(
            P("lat", "lev", None),
            P("lat", "lev", None),
            P("lat", None, "lev"),
            P("lat", None, "lev"),
        ),
        check_vma=False,
    )
```

time: 306 us -> 52.9 us (0.17)
  other arithmetic: 182 us -> 1.1 us
  local copies, waits for them, and re-layouts: 67 us -> 8.74 us
  matrix products: 23.4 us -> 0 us
  waiting for transfers between devices: 3.93 us -> 17 us
  starting transfers between devices: 26.4 us -> 17.2 us
  Pallas kernels: 0 us -> 7.7 us
    dynamic_update_slice x12 -> x0, other arithmetic: 168 us -> none  [hartley_table(): return lax.map(row_block, starts).reshape(lon_count, lon_count)]
    unnamed x18 -> x16, local copies, waits for them, and re-layouts: 37.2 us -> 7.77 us
    dot_general x6 -> x0, matrix products: 23.4 us -> none  [the longest x2 16.7 us: transform(): jnp.dot(values.reshape(-1, lon_count), hartley, preferred_element_type=jn...]
    all_to_all x2 -> x1, waiting for transfers between devices: 0.01 us -> 12.5 us  [per_device(): recv = lax.all_to_all(send, 'lev', split_axis=0, concat_axis=0, tiled=True)]
    all_to_all x2 -> x1, starting transfers between devices: 19.7 us -> 10.6 us  [per_device(): recv = lax.all_to_all(send, 'lev', split_axis=0, concat_axis=0, tiled=True)]
    all_to_all x3 -> x0, local copies, waits for them, and re-layouts: 8.84 us -> none  [the longest x2 4.68 us: per_device(): lax.all_to_all(thick_adv, 'lev', split_axis=2, concat_axis=1, tiled=True)]
    sub x2 -> x0, local copies, waits for them, and re-layouts: 8.71 us -> none  [advect(): field - (jnp.roll(flux_x, -1, axis=2) - flux_x) - (flux_y[1:] - flux_y[:-1])]
    add x15 -> x0, other arithmetic: 8.44 us -> none  [the longest x12 7.76 us: row_block(): row_ids = first_row + jnp.arange(block_size, dtype=jnp.int32)]
  transfers between devices with their start and end apart: 4 -> 3, of which waited for: 1 -> 3; matrix products, arithmetic and copies ran while one was open for 10% -> 0% of each run, Pallas kernels for 0% -> 0%
where the time goes in v1:
time: 52.9 us; the launch traced here: 52.4 us
  starting transfers between devices  17.2 us (33%)
  waiting for transfers between devices  17 us (32%)
  local copies, waits for them, and re-layouts  8.74 us (17%)
  Pallas kernels  7.7 us (15%)
  other arithmetic  1.1 us (2%)
  between operations  0.72 us (1%)
    all_to_all x1, waiting for transfers between devices, per_device(): recv = lax.all_to_all(send, 'lev', split_axis=0, concat_axis=0, tiled=True)  12.5 us
    all_to_all x1, starting transfers between devices, per_device(): recv = lax.all_to_all(send, 'lev', split_axis=0, concat_axis=0, tiled=True)  10.6 us
    unnamed x16, local copies, waits for them, and re-layouts  7.77 us
    pallas_call x1, Pallas kernels, per_device(): pl.pallas_call(functools.partial(filter_advect, lat_count), out_shape=(ja...  6.45 us
    ppermute x1, starting transfers between devices, per_device(): low = lax.ppermute(edge(lat_rows - 1), 'lat', forward)  4.59 us
    ppermute x1, waiting for transfers between devices, per_device(): high = lax.ppermute(edge(0), 'lat', backward)  4.4 us
    ppermute x1, starting transfers between devices, per_device(): high = lax.ppermute(edge(0), 'lat', backward)  1.92 us
    pallas_call x1, Pallas kernels, per_device(): pl.pallas_call(remap, out_shape=(out, out), compiler_params=pltpu.Compile...  1.26 us
  transfers between devices with their start and end apart: 3, of which 3 were waited for; matrix products, arithmetic and copies ran while one was open for 0% of the time, Pallas kernels for 0%

profile of v1, /device:TPU:1, one launch (start us, length us, event | category | flops | bytes accessed | tf_op | source)
XLA Modules:
  0.0 52.4 jit_solution(10277013936329689530)
XLA Ops:
  0.6 0.0 copy-start.6
  0.6 0.0 copy-start.7
  0.7 1.1 %multiply_convert_fusion = (bf16[1,8,2880]{2,1,0:T(8,128)(2,1)S(1)}, bf16[1,8,2880]{2,1,0:T(8,128)(2,1)S(1)}) fusion(f32[4,8,2880]{2,1,0:T(8,128)} %tracer_ref.1, f32[4,8,2880]{2,1,0:T(8,128)} %thick_ref.1), kind=kLoop, calls=%fused_computation.2 | loop fusion | flops 92160 | bytes 460800 | tf_op jit(solution)/shard_map/convert_element_type | solution.py:339
  1.7 1.0 %fusion = (bf16[1,8,2880]{2,1,0:T(8,128)(2,1)S(1)}, bf16[1,8,2880]{2,1,0:T(8,128)(2,1)S(1)}, bf16[1,8,2880]{2,1,0:T(8,128)(2,1)S(1)}, bf16[1,8,2880]{2,1,0:T(8,128)(2,1)S(1)}) fusion(f32[4,8,2880]{2,1,0:T(8,128)} %thick_ref.1, bf16[4,8,2880]{2,1,0:T(8,128)(2,1)} %v_ref.1), kind=kLoop, calls=%fused_computation.8 | loop fusion | bytes 368640 | tf_op jit(solution)/shard_map/slice | solution.py:337
  2.7 4.6 %collective-permute-start = (bf16[3,8,2880]{2,1,0:T(8,128)(2,1)S(1)}, bf16[3,8,2880]{2,1,0:T(8,128)(2,1)S(1)}, u32[]{:S(2)}, u32[]{:S(2)}) collective-permute-start(bf16[3,8,2880]{2,1,0:T(8,128)(2,1)S(1)} %pad_maximum_fusion), channel_id=1, source_target_pairs={{0,8},{8,16},{16,24},{24,32},{32,40},{40,48},{48,56},{56,64},{64,7... | collective-permute-start | bytes 414728 | tf_op jit(solution)/shard_map/ppermute | solution.py:343
  7.3 1.9 %collective-permute-start.1 = (bf16[3,8,2880]{2,1,0:T(8,128)(2,1)S(1)}, bf16[3,8,2880]{2,1,0:T(8,128)(2,1)S(1)}, u32[]{:S(2)}, u32[]{:S(2)}) collective-permute-start(bf16[3,8,2880]{2,1,0:T(8,128)(2,1)S(1)} %pad_maximum_fusion.1), channel_id=1, source_target_pairs={{8,0},{16,8},{24,16},{32,24},{40,32},{48,40},{56,48},{64,56},{72,6... | collective-permute-start | bytes 414728 | tf_op jit(solution)/shard_map/ppermute | solution.py:344
  9.3 0.1 collective-permute-done.low_ref
  9.3 4.4 %collective-permute-done.1.high_ref = bf16[3,8,2880]{2,1,0:T(8,128)(2,1)S(1)} collective-permute-done((bf16[3,8,2880]{2,1,0:T(8,128)(2,1)S(1)}, bf16[3,8,2880]{2,1,0:T(8,128)(2,1)S(1)}, u32[]{:S(2)}, u32[]{:S(2)}) %collective-permute-start.1) | collective-permute-done | bytes 138272 | tf_op jit(solution)/shard_map/ppermute | solution.py:344
  13.7 0.0 copy-start
  13.7 3.0 %copy-done = bf16[1536,2304]{1,0:T(8,128)(2,1)S(1)} copy-done((bf16[1536,2304]{1,0:T(8,128)(2,1)S(1)}, bf16[1536,2304]{1,0:T(8,128)(2,1)}, u32[]{:S(2)}) %copy-start) | copy-done | bytes 7077912
  16.7 0.0 copy-start.1
  16.7 1.0 %copy-done.1 = f32[4,8,2880]{2,1,0:T(8,128)S(1)} copy-done((f32[4,8,2880]{2,1,0:T(8,128)S(1)}, f32[4,8,2880]{2,1,0:T(8,128)}, u32[]{:S(2)}) %copy-start.1) | copy-done | bytes 368664
  17.7 0.0 copy-start.2
  17.7 1.0 %copy-done.2 = f32[4,8,2880]{2,1,0:T(8,128)S(1)} copy-done((f32[4,8,2880]{2,1,0:T(8,128)S(1)}, f32[4,8,2880]{2,1,0:T(8,128)}, u32[]{:S(2)}) %copy-start.2) | copy-done | bytes 368664
  18.7 0.0 copy-start.3
  18.7 0.9 %copy-done.3 = bf16[4,8,2880]{2,1,0:T(8,128)(2,1)S(1)} copy-done((bf16[4,8,2880]{2,1,0:T(8,128)(2,1)S(1)}, bf16[4,8,2880]{2,1,0:T(8,128)(2,1)}, u32[]{:S(2)}) %copy-start.3) | copy-done | bytes 184344
  19.7 0.9 %copy-done.4 = f32[17,1,3072]{2,1,0:T(1,128)S(1)} copy-done((f32[17,1,3072]{2,1,0:T(1,128)S(1)}, f32[17,1,3072]{2,1,0:T(1,128)}, u32[]{:S(2)}) %copy-start.4) | copy-done | bytes 208920
  20.6 0.9 %copy-done.5 = bf16[4,8,2880]{2,1,0:T(8,128)(2,1)S(1)} copy-done((bf16[4,8,2880]{2,1,0:T(8,128)(2,1)S(1)}, bf16[4,8,2880]{2,1,0:T(8,128)(2,1)}, u32[]{:S(2)}) %copy-start.5) | copy-done | bytes 184344
  21.5 6.4 %filter_advect.1 = (bf16[4,8,2880]{2,1,0:T(8,128)(2,1)}, bf16[4,8,2880]{2,1,0:T(8,128)(2,1)}, bf16[8,64,384]{2,1,0:T(8,128)(2,1)}) custom-call(bf16[4,8,2880]{2,1,0:T(8,128)(2,1)S(1)} %copy-done.5, bf16[4,8,2880]{2,1,0:T(8,128)(2,1)S(1)} %copy-done.3, f32[4,8,2880]{2,1,0:T(8,128)S(1)} %copy-done.1, f32[4,8,2880]{2,1,0:T(8,128)S(1)} %copy-done.2, ...), custom_call_target="tpu_custom_call" | custom-call | tf_op jit(solution)/shard_map/filter_advect/pallas_call | solution.py:346
  28.0 10.6 %all-to-all-start = ((bf16[8,64,384]{2,1,0:T(8,128)(2,1)}), bf16[8,64,384]{2,1,0:T(8,128)(2,1)S(1)}, u32[]{:S(2)}, u32[]{:S(2)}) async-start(bf16[8,64,384]{2,1,0:T(8,128)(2,1)} %get-tuple-element.11), calls=%async_computation | async-start | bytes 786432 | tf_op jit(solution)/shard_map/all_to_all | solution.py:364
  38.6 0.0 copy-done.6
  38.6 0.0 copy-done.7
  38.6 12.5 %all-to-all-done.recv_ref = bf16[8,64,384]{2,1,0:T(8,128)(2,1)S(1)} async-done(((bf16[8,64,384]{2,1,0:T(8,128)(2,1)}), bf16[8,64,384]{2,1,0:T(8,128)(2,1)S(1)}, u32[]{:S(2)}, u32[]{:S(2)}) %all-to-all-start) | async-done | bytes 393248 | tf_op jit(solution)/shard_map/all_to_all | solution.py:364
  51.2 1.3 %remap.1 = (f32[4,64,360]{2,1,0:T(8,128)}, f32[4,64,360]{2,1,0:T(8,128)}) custom-call(s32[1,128]{1,0:T(1,128)S(1)} %pad_bitcast_fusion.1.index_ref, f32[1,128]{1,0:T(1,128)S(1)} %pad_bitcast_fusion.frac_ref, bf16[8,64,384]{2,1,0:T(8,128)(2,1)S(1)} %all-to-all-done.recv_ref), custom_call_target="tpu_custom_call" | custom-call | tf_op jit(solution)/shard_map/remap/pallas_call | solution.py:369
  (6 shorter events, 0.1 us)
Async XLA Ops:
  0.6 38.0 %copy-start.6 = (s32[65]{0:T(128)S(1)}, s32[65]{0:T(128)}, u32[]{:S(2)}) copy-start(s32[65]{0:T(128)} %param.12) | copy-start | bytes 784
  0.6 38.0 %copy-start.7 = (f32[65]{0:T(128)S(1)}, f32[65]{0:T(128)}, u32[]{:S(2)}) copy-start(f32[65]{0:T(128)} %param.13) | copy-start | bytes 784
  2.7 6.6 %collective-permute-start = (bf16[3,8,2880]{2,1,0:T(8,128)(2,1)S(1)}, bf16[3,8,2880]{2,1,0:T(8,128)(2,1)S(1)}, u32[]{:S(2)}, u32[]{:S(2)}) collective-permute-start(bf16[3,8,2880]{2,1,0:T(8,128)(2,1)S(1)} %pad_maximum_fusion), channel_id=1, source_target_pairs={{0,8},{8,16},{16,24},{24,32},{32,40},{40,48},{48,56},{56,64},{64,7... | collective-permute-start | bytes 414728 | tf_op jit(solution)/shard_map/ppermute | solution.py:343
  7.3 6.4 %collective-permute-start.1 = (bf16[3,8,2880]{2,1,0:T(8,128)(2,1)S(1)}, bf16[3,8,2880]{2,1,0:T(8,128)(2,1)S(1)}, u32[]{:S(2)}, u32[]{:S(2)}) collective-permute-start(bf16[3,8,2880]{2,1,0:T(8,128)(2,1)S(1)} %pad_maximum_fusion.1), channel_id=1, source_target_pairs={{8,0},{16,8},{24,16},{32,24},{40,32},{48,40},{56,48},{64,56},{72,6... | collective-permute-start | bytes 414728 | tf_op jit(solution)/shard_map/ppermute | solution.py:344
  13.7 3.0 %copy-start = (bf16[1536,2304]{1,0:T(8,128)(2,1)S(1)}, bf16[1536,2304]{1,0:T(8,128)(2,1)}, u32[]{:S(2)}) copy-start(bf16[1536,2304]{1,0:T(8,128)(2,1)} %constant.8.clone.table_ref) | copy-start | bytes 21233668
  16.7 1.0 %copy-start.1 = (f32[4,8,2880]{2,1,0:T(8,128)S(1)}, f32[4,8,2880]{2,1,0:T(8,128)}, u32[]{:S(2)}) copy-start(f32[4,8,2880]{2,1,0:T(8,128)} %thick_ref.1) | copy-start | bytes 1105924
  17.7 1.0 %copy-start.2 = (f32[4,8,2880]{2,1,0:T(8,128)S(1)}, f32[4,8,2880]{2,1,0:T(8,128)}, u32[]{:S(2)}) copy-start(f32[4,8,2880]{2,1,0:T(8,128)} %tracer_ref.1) | copy-start | bytes 1105924
  18.7 0.9 %copy-start.3 = (bf16[4,8,2880]{2,1,0:T(8,128)(2,1)S(1)}, bf16[4,8,2880]{2,1,0:T(8,128)(2,1)}, u32[]{:S(2)}) copy-start(bf16[4,8,2880]{2,1,0:T(8,128)(2,1)} %v_ref.1) | copy-start | bytes 552964
  19.7 0.9 %copy-start.4 = (f32[17,1,3072]{2,1,0:T(1,128)S(1)}, f32[17,1,3072]{2,1,0:T(1,128)}, u32[]{:S(2)}) copy-start(f32[17,1,3072]{2,1,0:T(1,128)} %constant.9.clone.damp_ref) | copy-start | bytes 626692
  20.6 0.9 %copy-start.5 = (bf16[4,8,2880]{2,1,0:T(8,128)(2,1)S(1)}, bf16[4,8,2880]{2,1,0:T(8,128)(2,1)}, u32[]{:S(2)}) copy-start(bf16[4,8,2880]{2,1,0:T(8,128)(2,1)} %u_ref.1) | copy-start | bytes 552964
  28.0 23.2 %all-to-all-start = ((bf16[8,64,384]{2,1,0:T(8,128)(2,1)}), bf16[8,64,384]{2,1,0:T(8,128)(2,1)S(1)}, u32[]{:S(2)}, u32[]{:S(2)}) async-start(bf16[8,64,384]{2,1,0:T(8,128)(2,1)} %get-tuple-element.11), calls=%async_computation | async-start | bytes 786432 | tf_op jit(solution)/shard_map/all_to_all | solution.py:364

commit v2 on v1

--- a/solution.py
+++ b/solution.py
@@ -63,25 +63,90 @@
     return tables, damping
 
 
+def distance(lat, lat_count):
+    return jnp.minimum(lat, lat_count - 1 - lat)
+
+
+def is_polar(lat, lat_count):
+    d = distance(lat, lat_count)
+    return jnp.logical_and(d >= 0, 15 * d < 2 * (lat_count - 1))
+
+
+def band_is_polar(first_lat, lat_rows, lat_count):
+    found = is_polar(first_lat, lat_count)
+    for offset in (-1, lat_rows - 1, lat_rows):
+        found = jnp.logical_or(found, is_polar(first_lat + offset, lat_count))
+    return found
+
+
+def pack(v_hbm, thick_hbm, tracer_hbm, near_out, next_out, v_buf, thick_buf, tracer_buf, sems):
+    lat_rows = v_hbm.shape[0]
+    copies = []
+    for side, row in enumerate((0, lat_rows - 1)):
+        for source, target in ((v_hbm, v_buf), (thick_hbm, thick_buf), (tracer_hbm, tracer_buf)):
+            copy = pltpu.make_async_copy(source.at[row], target.at[side], sems.at[len(copies)])
+            copy.start()
+            copies.append(copy)
+    for copy in copies:
+        copy.wait()
+    odd = lax.axis_index("lat") % 2
+    for out, side in ((near_out, 1 - odd), (next_out, odd)):
+        thick = thick_buf[side]
+        out[0] = v_buf[side]
+        out[1] = thick.astype(jnp.bfloat16)
+        out[2] = (tracer_buf[side] * thick).astype(jnp.bfloat16)
+
+
+def load(lat_count, *refs):
+    sems = refs[-1]
+    half = len(refs) // 2
+    sources, targets = refs[:half], refs[half:-1]
+    always = len(sources) - 2
+    lat_rows = sources[0].shape[0]
+    copies = [
+        pltpu.make_async_copy(source, target, sems.at[place])
+        for place, (source, target) in enumerate(zip(sources, targets))
+    ]
+    polar = band_is_polar(lax.axis_index("lat") * lat_rows, lat_rows, lat_count)
+
+    @pl.when(polar)
+    def _():
+        for copy in copies[always:]:
+            copy.start()
+
+    for copy in copies[:always]:
+        copy.start()
+    for copy in copies[:always]:
+        copy.wait()
+
+    @pl.when(polar)
+    def _():
+        for copy in copies[always:]:
+            copy.wait()
+
+
 def filter_advect(
     lat_count,
     u_ref,
     v_ref,
     thick_ref,
     tracer_ref,
-    low_ref,
-    high_ref,
     table_ref,
     damp_ref,
+    near_ref,
+    next_ref,
+    u_hbm,
+    v_hbm,
+    send_ref,
     u_out,
     v_out,
-    send_ref,
     real_ref,
     work_ref,
     split_ref,
     prod_ref,
     spec_ref,
     edge_ref,
+    sems,
 ):
     lat_rows, level_rows, lon_count = u_ref.shape
     sectors = send_ref.shape[0]
@@ -95,22 +160,18 @@
     parts, columns = filter_parts(lon_count)
     places = table_places(parts)
 
-    def distance(lat):
-        return jnp.minimum(lat, lat_count - 1 - lat)
-
-    def is_polar(lat):
-        return jnp.logical_and(distance(lat) >= 0, 15 * distance(lat) < 2 * (lat_count - 1))
-
-    edge_ref[0] = low_ref[0].astype(f32)
-    edge_ref[1] = high_ref[0].astype(f32)
+    odd_device = lax.axis_index("lat") % 2
+    for side in range(2):
+        for source, odd in ((near_ref, 1 - side), (next_ref, side)):
+
+            @pl.when(odd_device == odd)
+            def _():
+                edge_ref[side] = source[...].astype(f32)
+
     u_out[...] = u_ref[...]
     v_out[...] = v_ref[...]
 
-    needs_filter = is_polar(first_lat)
-    for offset in (-1, lat_rows - 1, lat_rows):
-        needs_filter = jnp.logical_or(needs_filter, is_polar(first_lat + offset))
-
-    @pl.when(needs_filter)
+    @pl.when(band_is_polar(first_lat, lat_rows, lat_count))
     def _():
         half, quarter, eighth = parts[0][2], parts[1][2], parts[2][2]
         half_wide, quarter_wide, eighth_wide = (padded_to(part[2]) for part in parts[:3])
@@ -122,7 +183,7 @@
             elif g < 2 * lat_rows:
                 wind = v_ref[g - lat_rows].astype(f32)
             else:
-                wind = edge_ref[g - 2 * lat_rows]
+                wind = edge_ref[g - 2 * lat_rows, 0]
             real_ref[g, :, lon_count:] = jnp.zeros((level_rows, padded - lon_count), f32)
             real_ref[g, :, :lon_count] = wind
             near = real_ref[g, :, :half_wide]
@@ -153,7 +214,7 @@
                     prod_ref[start : start + level_rows, :]
                     + prod_ref[start + level_rows : start + 2 * level_rows, :]
                 )
-                place = jnp.clip(distance(lats[member]), 0, distances - 1)
+                place = jnp.clip(distance(lats[member], lat_count), 0, distances - 1)
                 pair.append(spectra * damp_ref[place])
             spec_ref[level_rows * g : level_rows * (g + 2), :] = jnp.concatenate(
                 pair, axis=0
@@ -184,16 +245,23 @@
         for g in range(2 * lat_rows):
             out = u_out if g < lat_rows else v_out
 
-            @pl.when(is_polar(lats[g]))
+            @pl.when(is_polar(lats[g], lat_count))
             def _():
                 out[g % lat_rows] = real_ref[g, :, :lon_count].astype(bf16)
 
         for side in range(2):
 
-            @pl.when(is_polar(lats[2 * lat_rows + side]))
+            @pl.when(is_polar(lats[2 * lat_rows + side], lat_count))
             def _():
                 smooth = real_ref[2 * lat_rows + side, :, :lon_count]
-                edge_ref[side] = smooth.astype(bf16).astype(f32)
+                edge_ref[side, 0] = smooth.astype(bf16).astype(f32)
+
+    winds_out = [
+        pltpu.make_async_copy(u_out, u_hbm, sems.at[0]),
+        pltpu.make_async_copy(v_out, v_hbm, sems.at[1]),
+    ]
+    for copy in winds_out:
+        copy.start()
 
     whole = lon_count // LANES * LANES
     rest = lon_count - whole
@@ -222,8 +290,8 @@
         real_ref[index, :, :lon_count] = value
         return real_ref[index]
 
-    fields_below = (low_ref[1].astype(f32), low_ref[2].astype(f32))
-    courant_below = courant(edge_ref[0])
+    fields_below = (edge_ref[0, 1], edge_ref[0, 2])
+    courant_below = courant(edge_ref[0, 0])
     flux_below = None
     for j in range(lat_rows):
         thick = thick_ref[j]
@@ -237,9 +305,8 @@
                 for below, here in zip(fields_below, (thick, mass))
             ]
         if j == lat_rows - 1:
-            courant_above = courant(edge_ref[1])
-            thick_above = high_ref[1].astype(f32)
-            mass_above = high_ref[2].astype(f32)
+            courant_above = courant(edge_ref[1, 0])
+            thick_above, mass_above = edge_ref[1, 1], edge_ref[1, 2]
         else:
             courant_above = courant(v_out[j + 1].astype(f32))
             thick_above = thick_ref[j + 1]
@@ -266,9 +333,13 @@
             block = both[:, s * sector : s * sector + sector_wide]
             send_ref[s, 2 * level_rows * j : 2 * level_rows * (j + 1), :] = block.astype(bf16)
         flux_below = flux_above
-
-
-def remap(index_ref, frac_ref, recv_ref, thick_out, tracer_out):
+    for copy in winds_out:
+        copy.wait()
+
+
+def remap(
+    index_ref, frac_ref, recv_ref, thick_hbm, tracer_hbm, thick_out, tracer_out, sems
+):
     lat_rows, level_count, sector = thick_out.shape
     sources, _, wide = recv_ref.shape
     level_rows = level_count // sources
@@ -292,6 +363,7 @@
     below, here, above = column(1.0 - inner), column(inner_next - outer), column(outer_next)
     place = lax.broadcasted_iota(jnp.int32, (level_rows, wide), 0)
     top, bottom = place == 0, place == level_rows - 1
+    copies = []
     for j in range(lat_rows):
         blocks = [
             recv_ref[source, 2 * level_rows * j : 2 * level_rows * (j + 1), :].astype(f32)
@@ -318,6 +390,12 @@
             thick, mass = results[0][source], results[1][source]
             thick_out[j, chosen, :] = thick[:, :sector]
             tracer_out[j, chosen, :] = (mass / thick)[:, :sector]
+        for source, target in ((thick_out, thick_hbm), (tracer_out, tracer_hbm)):
+            copy = pltpu.make_async_copy(source.at[j], target.at[j], sems.at[len(copies)])
+            copy.start()
+            copies.append(copy)
+    for copy in copies:
+        copy.wait()
 
 
 def per_device(u_wind, v_wind, thickness, tracer, remap_index, remap_frac):
@@ -333,43 +411,85 @@
     padded = (lon_count // LANES + 2) * LANES
     f32, bf16 = jnp.float32, jnp.bfloat16
 
-    def edge(row):
-        thick = thickness[row]
-        mass = tracer[row] * thick
-        return jnp.stack([v_wind[row], thick.astype(bf16), mass.astype(bf16)])
-
-    forward = [(i, i + 1) for i in range(lat_devices - 1)]
-    backward = [(target, source) for source, target in forward]
-    low = lax.ppermute(edge(lat_rows - 1), "lat", forward)
-    high = lax.ppermute(edge(0), "lat", backward)
+    in_hbm = pl.BlockSpec(memory_space=pltpu.HBM)
+    in_vmem = pl.BlockSpec(memory_space=pltpu.VMEM)
+    limit = pltpu.CompilerParams(vmem_limit_bytes=40 * 1024 * 1024)
+    edges = (3, level_rows, lon_count)
+
+    def stay(array):
+        return pltpu.with_memory_space_constraint(jnp.asarray(array), pltpu.HBM)
+
+    near, beyond = pl.pallas_call(
+        pack,
+        out_shape=(pltpu.VMEM(edges, bf16), pltpu.VMEM(edges, bf16)),
+        in_specs=[in_hbm] * 3,
+        out_specs=(in_vmem, in_vmem),
+        scratch_shapes=[
+            pltpu.VMEM((2, level_rows, lon_count), bf16),
+            pltpu.VMEM((2, level_rows, lon_count), f32),
+            pltpu.VMEM((2, level_rows, lon_count), f32),
+            pltpu.SemaphoreType.DMA((6,)),
+        ],
+        compiler_params=limit,
+        name="pack",
+    )(*(stay(array) for array in (v_wind, thickness, tracer)))
+    swap_near = [(i, i ^ 1) for i in range(lat_devices)]
+    swap_next = [(i, i - 1 + 2 * (i % 2)) for i in range(1, lat_devices - 1)]
+    beyond = lax.ppermute(beyond, "lat", swap_next)
+    near = lax.ppermute(near, "lat", swap_near)
+
+    arrays = (u_wind, v_wind, thickness, tracer, tables, damping)
+    moved_bytes = sum(array.size * array.dtype.itemsize for array in arrays)
+    loaded = pl.pallas_call(
+        functools.partial(load, lat_count),
+        out_shape=[pltpu.VMEM(array.shape, array.dtype) for array in arrays],
+        in_specs=[in_hbm] * len(arrays),
+        out_specs=[in_vmem] * len(arrays),
+        scratch_shapes=[pltpu.SemaphoreType.DMA((len(arrays),))],
+        compiler_params=limit,
+        cost_estimate=pl.CostEstimate(flops=0, bytes_accessed=moved_bytes, transcendentals=0),
+        name="load",
+    )(*(stay(array) for array in arrays))
     groups = 2 * lat_rows + 2
     u_filtered, v_filtered, send = pl.pallas_call(
         functools.partial(filter_advect, lat_count),
         out_shape=(
-            jax.ShapeDtypeStruct(u_wind.shape, bf16),
-            jax.ShapeDtypeStruct(v_wind.shape, bf16),
-            jax.ShapeDtypeStruct((sectors, 2 * lat_rows * level_rows, sector_wide), bf16),
+            pltpu.HBM(u_wind.shape, bf16),
+            pltpu.HBM(v_wind.shape, bf16),
+            pltpu.VMEM((sectors, 2 * lat_rows * level_rows, sector_wide), bf16),
         ),
+        in_specs=[in_vmem] * (len(arrays) + 2),
+        out_specs=(in_hbm, in_hbm, in_vmem),
         scratch_shapes=[
+            pltpu.VMEM(u_wind.shape, bf16),
+            pltpu.VMEM(v_wind.shape, bf16),
             pltpu.VMEM((groups, level_rows, padded), f32),
             pltpu.VMEM((groups, level_rows, padded), f32),
             pltpu.VMEM((2 * groups * level_rows, columns), bf16),
             pltpu.VMEM((2 * groups * level_rows, columns), f32),
             pltpu.VMEM((groups * level_rows, columns), bf16),
-            pltpu.VMEM((2, level_rows, lon_count), f32),
+            pltpu.VMEM((2, 3, level_rows, lon_count), f32),
+            pltpu.SemaphoreType.DMA((2,)),
         ],
-        compiler_params=pltpu.CompilerParams(vmem_limit_bytes=40 * 1024 * 1024),
+        compiler_params=limit,
         name="filter_advect",
-    )(u_wind, v_wind, thickness, tracer, low, high, tables, damping)
+    )(*loaded, near, beyond)
     recv = lax.all_to_all(send, "lev", split_axis=0, concat_axis=0, tiled=True)
     spare = -(level_count + 1) % LANES
     index_row = jnp.pad(remap_index, (0, spare))[None, :]
     frac_row = jnp.pad(remap_frac, (0, spare))[None, :]
-    out = jax.ShapeDtypeStruct((lat_rows, level_count, sector), f32)
+    shape = (lat_rows, level_count, sector)
     thick_out, tracer_out = pl.pallas_call(
         remap,
-        out_shape=(out, out),
-        compiler_params=pltpu.CompilerParams(vmem_limit_bytes=32 * 1024 * 1024),
+        out_shape=(pltpu.HBM(shape, f32), pltpu.HBM(shape, f32)),
+        in_specs=[in_vmem] * 3,
+        out_specs=(in_hbm, in_hbm),
+        scratch_shapes=[
+            pltpu.VMEM(shape, f32),
+            pltpu.VMEM(shape, f32),
+            pltpu.SemaphoreType.DMA((2 * lat_rows,)),
+        ],
+        compiler_params=limit,
         name="remap",
     )(index_row, frac_row, recv)
     return u_filtered, v_filtered, thick_out, tracer_out

time: 52.9 us -> 42.4 us (0.80)
  local copies, waits for them, and re-layouts: 8.74 us -> 0.01 us
  Pallas kernels: 7.7 us -> 12.7 us
  starting transfers between devices: 17.2 us -> 14.3 us
  waiting for transfers between devices: 17 us -> 14.3 us
  other arithmetic: 1.1 us -> 0 us
    unnamed x16 -> x4, local copies, waits for them, and re-layouts: 7.77 us -> 0.01 us
    pallas_call x2 -> x4, Pallas kernels: 7.7 us -> 12.7 us  [the longest x1 6.92 us: per_device(): pl.pallas_call(functools.partial(filter_advect, lat_count), out_shape=(pl...]
    ppermute x2, waiting for transfers between devices: 4.47 us -> 1.09 us  [the longest x1 1.09 us: per_device(): beyond = lax.ppermute(beyond, 'lat', swap_next)]
    all_to_all x1, starting transfers between devices: 10.6 us -> 8.95 us  [per_device(): recv = lax.all_to_all(send, 'lev', split_axis=0, concat_axis=0, tiled=True)]
    ppermute x2, starting transfers between devices: 6.52 us -> 5.37 us  [the longest x1 3.33 us: per_device(): near = lax.ppermute(near, 'lat', swap_near)]
    convert_element_type x1 -> x0, other arithmetic: 1.06 us -> none  [edge(): return jnp.stack([v_wind[row], thick.astype(bf16), mass.astype(bf16)])]
    slice x1 -> x0, local copies, waits for them, and re-layouts: 0.96 us -> none  [edge(): thick = thickness[row]]
    all_to_all x1, waiting for transfers between devices: 12.5 us -> 13.2 us  [per_device(): recv = lax.all_to_all(send, 'lev', split_axis=0, concat_axis=0, tiled=True)]
  transfers between devices with their start and end apart: 3 -> 3, of which waited for: 3 -> 2; matrix products, arithmetic and copies ran while one was open for 0% -> 0% of each run, Pallas kernels for 0% -> 8%
where the time goes in v2:
time: 42.4 us; the launch traced here: 42.1 us
  starting transfers between devices  14.3 us (34%)
  waiting for transfers between devices  14.3 us (34%)
  Pallas kernels  12.7 us (30%)
  between operations  0.7 us (2%)
    all_to_all x1, waiting for transfers between devices, per_device(): recv = lax.all_to_all(send, 'lev', split_axis=0, concat_axis=0, tiled=True)  13.2 us
    all_to_all x1, starting transfers between devices, per_device(): recv = lax.all_to_all(send, 'lev', split_axis=0, concat_axis=0, tiled=True)  8.95 us
    pallas_call x1, Pallas kernels, per_device(): pl.pallas_call(functools.partial(filter_advect, lat_count), out_shape=(pl...  6.92 us
    pallas_call x1, Pallas kernels, per_device(): pl.pallas_call(functools.partial(load, lat_count), out_shape=[pltpu.VMEM(...  3.36 us
    ppermute x1, starting transfers between devices, per_device(): near = lax.ppermute(near, 'lat', swap_near)  3.33 us
    ppermute x1, starting transfers between devices, per_device(): beyond = lax.ppermute(beyond, 'lat', swap_next)  2.04 us
    pallas_call x1, Pallas kernels, per_device(): pl.pallas_call(remap, out_shape=(pltpu.HBM(shape, f32), pltpu.HBM(shape,...  1.31 us
    pallas_call x1, Pallas kernels, per_device(): pl.pallas_call(pack, out_shape=(pltpu.VMEM(edges, bf16), pltpu.VMEM(edges...  1.16 us
  transfers between devices with their start and end apart: 3, of which 2 were waited for; matrix products, arithmetic and copies ran while one was open for 0% of the time, Pallas kernels for 8%

profile of v2, /device:TPU:1, one launch (start us, length us, event | category | flops | bytes accessed | tf_op | source)
XLA Modules:
  0.0 42.1 jit_solution(1878763606766351964)
XLA Ops:
  0.6 1.2 %pack.1 = (bf16[3,8,2880]{2,1,0:T(8,128)(2,1)S(1)}, bf16[3,8,2880]{2,1,0:T(8,128)(2,1)S(1)}) custom-call(bf16[4,8,2880]{2,1,0:T(8,128)(2,1)} %v_hbm.1, f32[4,8,2880]{2,1,0:T(8,128)} %thick_hbm.1, f32[4,8,2880]{2,1,0:T(8,128)} %tracer_hbm.1), custom_call_target="tpu_custom_call" | custom-call | tf_op jit(solution)/shard_map/pack/pallas_call | solution.py:422
  1.8 3.3 %collective-permute-start = (bf16[3,8,2880]{2,1,0:T(8,128)(2,1)S(1)}, bf16[3,8,2880]{2,1,0:T(8,128)(2,1)S(1)}, u32[]{:S(2)}, u32[]{:S(2)}) collective-permute-start(bf16[3,8,2880]{2,1,0:T(8,128)(2,1)S(1)} %get-tuple-element.23), channel_id=1, source_target_pairs={{0,8},{8,0},{16,24},{24,16},{32,40},{40,32},{48,56},{56,48},{64,72... | collective-permute-start | bytes 414728 | tf_op jit(solution)/shard_map/ppermute | solution.py:439
  5.1 0.0 copy-start
  5.1 0.0 copy-start.1
  5.1 2.0 %collective-permute-start.1 = (bf16[3,8,2880]{2,1,0:T(8,128)(2,1)S(1)}, bf16[3,8,2880]{2,1,0:T(8,128)(2,1)S(1)}, u32[]{:S(2)}, u32[]{:S(2)}) collective-permute-start(bf16[3,8,2880]{2,1,0:T(8,128)(2,1)S(1)} %get-tuple-element.24), channel_id=1, source_target_pairs={{8,16},{16,8},{24,32},{32,24},{40,48},{48,40},{56,64},{64,56},{72,... | collective-permute-start | bytes 414728 | tf_op jit(solution)/shard_map/ppermute | solution.py:438
  7.2 3.4 %load.1 = (bf16[4,8,2880]{2,1,0:T(8,128)(2,1)S(1)}, bf16[4,8,2880]{2,1,0:T(8,128)(2,1)S(1)}, f32[4,8,2880]{2,1,0:T(8,128)S(1)}, f32[4,8,2880]{2,1,0:T(8,128)S(1)...) custom-call(bf16[4,8,2880]{2,1,0:T(8,128)(2,1)} %refs_0_.1, bf16[4,8,2880]{2,1,0:T(8,128)(2,1)} %v_hbm.1, ...), custom_call_target="tpu_custom_call" | custom-call | bytes 8392704 | tf_op jit(solution)/shard_map/load/pallas_call | solution.py:443
  10.5 0.0 collective-permute-done.near_ref
  10.6 1.1 %collective-permute-done.1.next_ref = bf16[3,8,2880]{2,1,0:T(8,128)(2,1)S(1)} collective-permute-done((bf16[3,8,2880]{2,1,0:T(8,128)(2,1)S(1)}, bf16[3,8,2880]{2,1,0:T(8,128)(2,1)S(1)}, u32[]{:S(2)}, u32[]{:S(2)}) %collective-permute-start.1) | collective-permute-done | bytes 138272 | tf_op jit(solution)/shard_map/ppermute | solution.py:438
  11.6 6.9 %filter_advect.1 = (bf16[4,8,2880]{2,1,0:T(8,128)(2,1)}, bf16[4,8,2880]{2,1,0:T(8,128)(2,1)}, bf16[8,64,384]{2,1,0:T(8,128)(2,1)}) custom-call(bf16[4,8,2880]{2,1,0:T(8,128)(2,1)S(1)} %get-tuple-element.17.u_ref, bf16[4,8,2880]{2,1,0:T(8,128)(2,1)S(1)} %get-tuple-element.18.v_ref, f32[4,8,2880]{2,1,0:T(8,128)S(1)} %get-tuple-element.19.thick_ref, ...), custom_call_target="tpu_custom_call" | custom-call | tf_op jit(solution)/shard_map/filter_advect/pallas_call | solution.py:454
  18.6 8.9 %all-to-all-start = ((bf16[8,64,384]{2,1,0:T(8,128)(2,1)}), bf16[8,64,384]{2,1,0:T(8,128)(2,1)S(1)}, u32[]{:S(2)}, u32[]{:S(2)}) async-start(bf16[8,64,384]{2,1,0:T(8,128)(2,1)} %get-tuple-element.27), calls=%async_computation | async-start | bytes 786432 | tf_op jit(solution)/shard_map/all_to_all | solution.py:477
  27.5 0.0 copy-done
  27.5 0.0 copy-done.1
  27.6 13.2 %all-to-all-done.recv_ref = bf16[8,64,384]{2,1,0:T(8,128)(2,1)S(1)} async-done(((bf16[8,64,384]{2,1,0:T(8,128)(2,1)}), bf16[8,64,384]{2,1,0:T(8,128)(2,1)S(1)}, u32[]{:S(2)}, u32[]{:S(2)}) %all-to-all-start) | async-done | bytes 393248 | tf_op jit(solution)/shard_map/all_to_all | solution.py:477
  40.8 1.3 %remap.1 = (f32[4,64,360]{2,1,0:T(8,128)}, f32[4,64,360]{2,1,0:T(8,128)}) custom-call(s32[1,128]{1,0:T(1,128)S(1)} %pad_bitcast_fusion.1.index_ref, f32[1,128]{1,0:T(1,128)S(1)} %pad_bitcast_fusion.frac_ref, bf16[8,64,384]{2,1,0:T(8,128)(2,1)S(1)} %all-to-all-done.recv_ref), custom_call_target="tpu_custom_call" | custom-call | tf_op jit(solution)/shard_map/remap/pallas_call | solution.py:482
  (2 shorter events, 0.0 us)
Async XLA Ops:
  1.8 8.7 %collective-permute-start = (bf16[3,8,2880]{2,1,0:T(8,128)(2,1)S(1)}, bf16[3,8,2880]{2,1,0:T(8,128)(2,1)S(1)}, u32[]{:S(2)}, u32[]{:S(2)}) collective-permute-start(bf16[3,8,2880]{2,1,0:T(8,128)(2,1)S(1)} %get-tuple-element.23), channel_id=1, source_target_pairs={{0,8},{8,0},{16,24},{24,16},{32,40},{40,32},{48,56},{56,48},{64,72... | collective-permute-start | bytes 414728 | tf_op jit(solution)/shard_map/ppermute | solution.py:439
  5.1 22.4 %copy-start = (f32[65]{0:T(128)S(1)}, f32[65]{0:T(128)}, u32[]{:S(2)}) copy-start(f32[65]{0:T(128)} %param.13) | copy-start | bytes 784
  5.1 22.4 %copy-start.1 = (s32[65]{0:T(128)S(1)}, s32[65]{0:T(128)}, u32[]{:S(2)}) copy-start(s32[65]{0:T(128)} %param.12) | copy-start | bytes 784
  5.1 6.5 %collective-permute-start.1 = (bf16[3,8,2880]{2,1,0:T(8,128)(2,1)S(1)}, bf16[3,8,2880]{2,1,0:T(8,128)(2,1)S(1)}, u32[]{:S(2)}, u32[]{:S(2)}) collective-permute-start(bf16[3,8,2880]{2,1,0:T(8,128)(2,1)S(1)} %get-tuple-element.24), channel_id=1, source_target_pairs={{8,16},{16,8},{24,32},{32,24},{40,48},{48,40},{56,64},{64,56},{72,... | collective-permute-start | bytes 414728 | tf_op jit(solution)/shard_map/ppermute | solution.py:438
  18.6 22.2 %all-to-all-start = ((bf16[8,64,384]{2,1,0:T(8,128)(2,1)}), bf16[8,64,384]{2,1,0:T(8,128)(2,1)S(1)}, u32[]{:S(2)}, u32[]{:S(2)}) async-start(bf16[8,64,384]{2,1,0:T(8,128)(2,1)} %get-tuple-element.27), calls=%async_computation | async-start | bytes 786432 | tf_op jit(solution)/shard_map/all_to_all | solution.py:477

commit v3 on v2

v3 whole, which is shorter than its diff:
```python
import functools
import math

import jax
import jax.numpy as jnp
import ml_dtypes
import numpy as np
from jax import lax
from jax.experimental import pallas as pl
from jax.experimental.pallas import tpu as pltpu
from jax.sharding import PartitionSpec as P

COS_EDGE = math.cos(66.0 * math.pi / 180.0)
LANES = 128
THICK_MID = 1.25


def padded_to(count):
    return -(-count // LANES) * LANES


def filter_parts(lon_count):
    parts = []
    column = 0
    for first, step, points in (
        (1, 2, lon_count // 2),
        (2, 4, lon_count // 4),
        (4, 8, lon_count // 8),
        (0, 8, lon_count // 8),
    ):
        parts.append((first, step, points, column))
        column += padded_to(points)
    return parts, column


def table_places(parts):
    odd, two, four, eight = (padded_to(part[2]) for part in parts)
    return [(0, 0, odd), (0, odd, two), (two, odd, four), (two, odd + four, eight)]


def filter_tables(lat_count, lon_count):
    phase = 2.0 * np.pi * np.arange(lon_count) / lon_count
    rounded = (np.cos(phase) + np.sin(phase)).astype(np.float32).astype(ml_dtypes.bfloat16)
    polar = [d for d in range((lat_count + 1) // 2) if 15 * d < 2 * (lat_count - 1)]
    ratio = (np.sin(np.pi * np.array(polar, np.float64) / (lat_count - 1)) / COS_EDGE) ** 2
    wave = np.arange(lon_count)
    wave = np.minimum(wave, lon_count - wave)
    sine_square = np.sin(np.pi * wave / lon_count) ** 2
    sine_square[0] = 1.0
    values = np.minimum(1.0, ratio[:, None] / sine_square[None, :])
    values[:, 0] = 1.0

    parts, columns = filter_parts(lon_count)
    places = table_places(parts)
    tables = np.zeros((places[0][2], places[0][2] + places[1][2]), ml_dtypes.bfloat16)
    damping = np.zeros((len(polar), 1, columns), np.float32)
    for (first, step, points, column), (row, left, _) in zip(parts, places):
        waves = first + step * np.arange(points)
        values_here = rounded[np.arange(points)[:, None] * waves[None, :] % lon_count]
        tables[row : row + points, left : left + points] = values_here
        damping[:, 0, column : column + points] = values[:, waves]
    return tables, damping


def distance(lat, lat_count):
    return jnp.minimum(lat, lat_count - 1 - lat)


def is_polar(lat, lat_count):
    d = distance(lat, lat_count)
    return jnp.logical_and(d >= 0, 15 * d < 2 * (lat_count - 1))


def band_is_polar(first_lat, lat_rows, lat_count):
    found = is_polar(first_lat, lat_count)
    for offset in (-1, lat_rows - 1, lat_rows):
        found = jnp.logical_or(found, is_polar(first_lat + offset, lat_count))
    return found


def pack(v_hbm, thick_hbm, tracer_hbm, near_out, next_out, v_buf, thick_buf, tracer_buf, sems):
    lat_rows = v_hbm.shape[0]
    copies = []
    for side, row in enumerate((0, lat_rows - 1)):
        for source, target in ((v_hbm, v_buf), (thick_hbm, thick_buf), (tracer_hbm, tracer_buf)):
            copy = pltpu.make_async_copy(source.at[row], target.at[side], sems.at[len(copies)])
            copy.start()
            copies.append(copy)
    for copy in copies:
        copy.wait()
    odd = lax.axis_index("lat") % 2
    for out, side in ((near_out, 1 - odd), (next_out, odd)):
        thick = thick_buf[side]
        out[0] = v_buf[side]
        out[1] = thick.astype(jnp.bfloat16)
        out[2] = (tracer_buf[side] * thick).astype(jnp.bfloat16)


def courant(wind):
    return jnp.clip(0.05 * wind, -0.15, 0.15)


def loop(count, body):
    def step(place, carry):
        body(place)
        return carry

    lax.fori_loop(0, count, step, 0)


def rows_at(place, count):
    return pl.ds(pl.multiple_of(place * count, count), count)


def up_and_down(face):
    return jnp.maximum(face, 0.0), jnp.minimum(face, 0.0)


def to_sectors(send_ref, moved_ref, j, sector):
    sectors, _, sector_wide = send_ref.shape
    height = moved_ref.shape[1]
    for s in range(sectors):
        block = moved_ref[j, :, s * sector : s * sector + sector_wide]
        send_ref[s, rows_at(j, height), :] = block.astype(send_ref.dtype)


def transport(j, wind_ref, row_ref, real_ref, moved_ref, least_face, most_face):
    level_rows, lon_count = row_ref.shape[2:]
    padded = real_ref.shape[2]
    whole = lon_count // LANES * LANES
    rest = lon_count - whole
    lane = lax.broadcasted_iota(jnp.int32, (level_rows, LANES), 1)

    def extend(index, value):
        real_ref[index, :, :lon_count] = value
        tail = jnp.where(
            lane < rest,
            real_ref[index, :, whole : whole + LANES],
            pltpu.roll(real_ref[index, :, :LANES], rest, 1),
        )
        ends = pltpu.roll(tail, LANES - rest, 1)
        real_ref[index, :, whole : whole + LANES] = tail
        real_ref[index, :, whole + LANES :] = ends
        return real_ref[index]

    def before(value):
        return pltpu.roll(value, 1, 1)

    def after(value):
        return pltpu.roll(value, padded - 1, 1)

    def face_y(f):
        face = 0.5 * (courant(row_ref[0, f]) + courant(row_ref[0, f + 1]))
        inside = jnp.logical_and(f >= least_face, f <= most_face)
        return up_and_down(face * jnp.where(inside, 1.0, 0.0))

    (rise_below, fall_below), (rise_above, fall_above) = face_y(j), face_y(j + 1)
    courant_x = extend(0, courant(wind_ref[j].astype(jnp.float32)))
    rise_x, fall_x = up_and_down(0.5 * (before(courant_x) + courant_x))
    for i in range(2):
        below, here, above = (row_ref[1 + i, j + k] for k in range(3))
        field = extend(1 + i, here)
        flux_x = rise_x * before(field) + fall_x * field
        across = rise_above * here + fall_above * above - rise_below * below - fall_below * here
        result = field - (after(flux_x) - flux_x)
        if i == 0:
            result = result - THICK_MID
        moved_ref[j, i * level_rows : (i + 1) * level_rows, :lon_count] = (
            result[:, :lon_count] - across
        )


def band_weights(index_ref, frac_ref, weight_ref):
    _, level_count, wide = weight_ref.shape

    def inner(k):
        return jnp.where(index_ref[k] == k, 1.0, frac_ref[k])

    def outer(k):
        return jnp.where(index_ref[k] == k, frac_ref[k], 0.0)

    def weigh(k):
        for place, weight in enumerate(
            (1.0 - inner(k), inner(k + 1) - outer(k), outer(k + 1))
        ):
            weight_ref[place, pl.ds(k, 1), :] = jnp.full((1, wide), weight, jnp.float32)

    loop(level_count, weigh)


def load(
    lat_count,
    index_hbm,
    frac_hbm,
    u_hbm,
    v_hbm,
    thick_hbm,
    tracer_hbm,
    table_hbm,
    damp_hbm,
    u_ref,
    v_ref,
    thick_ref,
    tracer_ref,
    table_ref,
    damp_ref,
    u_out,
    v_out,
    send_ref,
    moved_ref,
    weight_ref,
    row_ref,
    real_ref,
    index_ref,
    frac_ref,
    sems,
    table_sems,
):
    lat_rows, level_rows, lon_count = u_ref.shape
    f32 = jnp.float32
    polar = band_is_polar(lax.axis_index("lat") * lat_rows, lat_rows, lat_count)
    inputs = [
        pltpu.make_async_copy(source, target, sems.at[place])
        for place, (source, target) in enumerate(
            ((v_hbm, v_ref), (thick_hbm, thick_ref), (tracer_hbm, tracer_ref), (u_hbm, u_ref))
        )
    ]
    tables = [pltpu.make_async_copy(damp_hbm, damp_ref, sems.at[4])]
    chunks = table_sems.shape[0]
    height = table_hbm.shape[0] // chunks
    for chunk in range(chunks):
        part = pl.ds(chunk * height, height)
        tables.append(
            pltpu.make_async_copy(table_hbm.at[part], table_ref.at[part], table_sems.at[chunk])
        )
    for copy in inputs:
        copy.start()

    @pl.when(polar)
    def _():
        for copy in tables:
            copy.start()

    scalars = [
        pltpu.make_async_copy(index_hbm, index_ref, sems.at[7]),
        pltpu.make_async_copy(frac_hbm, frac_ref, sems.at[8]),
    ]
    for copy in scalars:
        copy.start()

    def weigh():
        for copy in scalars:
            copy.wait()
        band_weights(index_ref, frac_ref, weight_ref)

    @pl.when(polar)
    def _():
        weigh()
        for copy in inputs:
            copy.wait()
        for copy in tables:
            copy.wait()

    @pl.when(jnp.logical_not(polar))
    def _():
        for copy in inputs:
            copy.wait()
        winds = [
            pltpu.make_async_copy(u_ref, u_out, sems.at[5]),
            pltpu.make_async_copy(v_ref, v_out, sems.at[6]),
        ]
        for copy in winds:
            copy.start()
        blank = jnp.zeros((level_rows, lon_count), f32)
        for place in range(3):
            row_ref[place, 0] = blank
            row_ref[place, lat_rows + 1] = blank

        def prepare(j):
            thick = thick_ref[j]
            row_ref[0, j + 1] = v_ref[j].astype(f32)
            row_ref[1, j + 1] = thick
            row_ref[2, j + 1] = tracer_ref[j] * thick

        loop(lat_rows, prepare)

        def advect(j):
            transport(j, u_ref, row_ref, real_ref, moved_ref, 1, lat_rows - 1)

            @pl.when(jnp.logical_and(j > 0, j < lat_rows - 1))
            def _():
                to_sectors(send_ref, moved_ref, j, lon_count // send_ref.shape[0])

        loop(lat_rows, advect)
        weigh()
        for copy in winds:
            copy.wait()


def filter_advect(
    lat_count,
    u_ref,
    v_ref,
    thick_ref,
    tracer_ref,
    table_ref,
    damp_ref,
    partial_ref,
    near_ref,
    next_ref,
    u_held,
    v_held,
    send_held,
    u_hbm,
    v_hbm,
    send_ref,
    u_out,
    v_out,
    real_ref,
    work_ref,
    split_ref,
    prod_ref,
    spec_ref,
    row_ref,
    moved_ref,
    sems,
):
    lat_rows, level_rows, lon_count = u_ref.shape
    groups, _, padded = real_ref.shape
    distances = damp_ref.shape[0]
    first_lat = lax.axis_index("lat") * lat_rows
    f32 = jnp.float32
    bf16 = jnp.bfloat16
    parts, columns = filter_parts(lon_count)
    places = table_places(parts)
    odd_device = lax.axis_index("lat") % 2
    polar = band_is_polar(first_lat, lat_rows, lat_count)

    for side in range(2):
        for source, odd in ((near_ref, 1 - side), (next_ref, side)):

            @pl.when(odd_device == odd)
            def _():
                for place in range(3):
                    row_ref[place, side * (lat_rows + 1)] = source[place].astype(f32)

    @pl.when(jnp.logical_not(polar))
    def _():
        for side, j in enumerate((0, lat_rows - 1)):
            outer = side * (lat_rows + 1)
            own = courant(v_ref[j].astype(f32))
            face = 0.5 * (courant(row_ref[0, outer]) + own)
            at_pole = first_lat + side * lat_rows == side * lat_count
            rise, fall = up_and_down(face * jnp.where(at_pole, 0.0, 1.0))
            thick = thick_ref[j]
            for i, here in enumerate((thick, tracer_ref[j] * thick)):
                rows = slice(i * level_rows, (i + 1) * level_rows)
                if side:
                    value = partial_ref[j, rows, :lon_count] - (
                        rise * here + fall * row_ref[1 + i, outer]
                    )
                else:
                    value = partial_ref[j, rows, :lon_count] + (
                        rise * row_ref[1 + i, outer] + fall * here
                    )
                moved_ref[j, rows, :lon_count] = value
            to_sectors(send_ref, moved_ref, j, lon_count // send_ref.shape[0])

    @pl.when(polar)
    def _():
        def prepare(j):
            thick = thick_ref[j]
            row_ref[0, j + 1] = v_ref[j].astype(f32)
            row_ref[1, j + 1] = thick
            row_ref[2, j + 1] = tracer_ref[j] * thick
            u_out[j] = u_ref[j]
            v_out[j] = v_ref[j]

        loop(lat_rows, prepare)
        half, quarter, eighth = parts[0][2], parts[1][2], parts[2][2]
        half_wide, quarter_wide, eighth_wide = (padded_to(part[2]) for part in parts[:3])
        last = lat_rows + 2

        def lat_of(g):
            return first_lat + (g if g < lat_rows else g - lat_rows - 1)

        def fold(g, wind):
            real_ref[g, :, lon_count:] = jnp.zeros((level_rows, padded - lon_count), f32)
            real_ref[g, :, :lon_count] = wind
            near = real_ref[g, :, :half_wide]
            far = real_ref[g, :, half : half + half_wide]
            odd, even = near - far, near + far
            work_ref[g, :, :half_wide] = even
            near = even[:, :quarter_wide]
            far = work_ref[g, :, quarter : quarter + quarter_wide]
            two, even = near - far, near + far
            work_ref[g, :, half_wide : half_wide + quarter_wide] = even
            near = even[:, :eighth_wide]
            far = work_ref[g, :, half_wide + eighth : half_wide + eighth + eighth_wide]
            row = jnp.concatenate([odd, two, near - far, near + far], axis=1)
            high = row.astype(bf16).astype(f32)
            both = jnp.concatenate([high, row - high], axis=0)
            split_ref[rows_at(g, 2 * level_rows), :] = both.astype(bf16)

        for j in range(lat_rows):
            fold(j, u_ref[j].astype(f32))
        for j in range(last):
            fold(lat_rows + j, row_ref[0, j])

        for (_, _, _, column), (top, left, size) in zip(parts, places):
            prod_ref[:, column : column + size] = jnp.dot(
                split_ref[:, column : column + size],
                table_ref[top : top + size, left : left + size],
                preferred_element_type=f32,
            )

        for pair in range(groups // 2):
            values = []
            for g in (2 * pair, 2 * pair + 1):
                start = 2 * level_rows * g
                high = prod_ref[start : start + level_rows, :]
                low = prod_ref[start + level_rows : start + 2 * level_rows, :]
                place = jnp.clip(distance(lat_of(g), lat_count), 0, distances - 1)
                values.append((high + low) * damp_ref[place])
            spec_ref[2 * level_rows * pair : 2 * level_rows * (pair + 1), :] = jnp.concatenate(
                values, axis=0
            ).astype(bf16)
        rows = groups * level_rows

        for (_, _, _, column), (top, left, size) in zip(parts, places):
            prod_ref[:rows, column : column + size] = lax.dot_general(
                spec_ref[:, column : column + size],
                table_ref[top : top + size, left : left + size],
                (((1,), (1,)), ((), ())),
                preferred_element_type=f32,
            )

        for g in range(groups):
            start = level_rows * g
            odd, two, four, eight = (
                prod_ref[start : start + level_rows, column : column + padded_to(points)]
                for _, _, points, column in parts
            )
            work_ref[g, :, :eighth_wide] = eight + four
            work_ref[g, :, eighth : 2 * eighth] = (eight - four)[:, :eighth]
            even = work_ref[g, :, :quarter_wide]
            work_ref[g, :, :quarter_wide] = even + two
            work_ref[g, :, quarter : 2 * quarter] = (even - two)[:, :quarter]
            even = work_ref[g, :, :half_wide]
            scale = 1.0 / lon_count
            real_ref[g, :, :half_wide] = (even + odd) * scale
            real_ref[g, :, half : 2 * half] = ((even - odd) * scale)[:, :half]

        def finish(j):
            smooth = real_ref[lat_rows + j, :, :lon_count].astype(bf16)

            @pl.when(is_polar(first_lat + j - 1, lat_count))
            def _():
                row_ref[0, j] = smooth.astype(f32)

                @pl.when(jnp.logical_and(j > 0, j <= lat_rows))
                def _():
                    inner = jnp.clip(j - 1, 0, lat_rows - 1)
                    v_out[inner] = smooth
                    u_out[inner] = real_ref[inner, :, :lon_count].astype(bf16)

        loop(last, finish)

        winds_out = [
            pltpu.make_async_copy(u_out, u_hbm, sems.at[0]),
            pltpu.make_async_copy(v_out, v_hbm, sems.at[1]),
        ]
        for copy in winds_out:
            copy.start()
        least = jnp.where(first_lat == 0, 1, 0)
        most = jnp.where(first_lat + lat_rows == lat_count, lat_rows - 1, lat_rows)

        def advect(j):
            transport(j, u_out, row_ref, real_ref, moved_ref, least, most)
            to_sectors(send_ref, moved_ref, j, lon_count // send_ref.shape[0])

        loop(lat_rows, advect)
        for copy in winds_out:
            copy.wait()


def remap(weight_ref, recv_ref, thick_hbm, tracer_hbm, thick_out, tracer_out, sems):
    lat_rows, level_count, sector = thick_out.shape
    sources, _, wide = recv_ref.shape
    level_rows = level_count // sources
    f32 = jnp.float32
    below, here, above = (weight_ref[place] for place in range(3))
    place = lax.broadcasted_iota(jnp.int32, (level_rows, wide), 0)
    top, bottom = place == 0, place == level_rows - 1

    def results_out(j):
        return [
            pltpu.make_async_copy(source.at[j], target.at[j], sems.at[i, j])
            for i, (source, target) in enumerate(
                ((thick_out, thick_hbm), (tracer_out, tracer_hbm))
            )
        ]

    def work(j):
        blocks = [
            recv_ref[source, rows_at(j, 2 * level_rows), :].astype(f32)
            for source in range(sources)
        ]
        results = []
        for index in range(2):
            layers = [block[level_rows * index : level_rows * (index + 1)] for block in blocks]
            if index == 0:
                layers = [layer + THICK_MID for layer in layers]
            down = [pltpu.roll(layer, 1, 0) for layer in layers]
            up = [pltpu.roll(layer, level_rows - 1, 0) for layer in layers]
            outs = []
            for source in range(sources):
                chosen = slice(level_rows * source, level_rows * (source + 1))
                lower = jnp.where(top, down[max(source - 1, 0)], down[source])
                higher = jnp.where(bottom, up[min(source + 1, sources - 1)], up[source])
                outs.append(
                    below[chosen] * lower + here[chosen] * layers[source] + above[chosen] * higher
                )
            results.append(outs)
        for source in range(sources):
            chosen = slice(level_rows * source, level_rows * (source + 1))
            thick, mass = results[0][source], results[1][source]
            thick_out[j, chosen, :] = thick[:, :sector]
            tracer_out[j, chosen, :] = (mass / thick)[:, :sector]
        for copy in results_out(j):
            copy.start()

    loop(lat_rows, work)
    for j in range(lat_rows):
        for copy in results_out(j):
            copy.wait()


def per_device(u_wind, v_wind, thickness, tracer, remap_index, remap_frac):
    lat_rows, level_rows, lon_count = u_wind.shape
    lat_devices = lax.axis_size("lat")
    lat_count = lat_rows * lat_devices
    sectors = lax.axis_size("lev")
    level_count = level_rows * sectors
    sector = lon_count // sectors
    sector_wide = padded_to(sector)
    tables, damping = filter_tables(lat_count, lon_count)
    columns = damping.shape[2]
    padded = (lon_count // LANES + 2) * LANES
    f32, bf16 = jnp.float32, jnp.bfloat16

    in_hbm = pl.BlockSpec(memory_space=pltpu.HBM)
    in_vmem = pl.BlockSpec(memory_space=pltpu.VMEM)

    def limit(mebibytes):
        return pltpu.CompilerParams(vmem_limit_bytes=mebibytes * 1024 * 1024)

    edges = (3, level_rows, lon_count)

    def stay(array):
        return pltpu.with_memory_space_constraint(jnp.asarray(array), pltpu.HBM)

    near, beyond = pl.pallas_call(
        pack,
        out_shape=(pltpu.VMEM(edges, bf16), pltpu.VMEM(edges, bf16)),
        in_specs=[in_hbm] * 3,
        out_specs=(in_vmem, in_vmem),
        scratch_shapes=[
            pltpu.VMEM((2, level_rows, lon_count), bf16),
            pltpu.VMEM((2, level_rows, lon_count), f32),
            pltpu.VMEM((2, level_rows, lon_count), f32),
            pltpu.SemaphoreType.DMA((6,)),
        ],
        compiler_params=limit(8),
        name="pack",
    )(*(stay(array) for array in (v_wind, thickness, tracer)))
    swap_near = [(i, i ^ 1) for i in range(lat_devices)]
    swap_next = [(i, i - 1 + 2 * (i % 2)) for i in range(1, lat_devices - 1)]
    near = lax.ppermute(near, "lat", swap_near)
    beyond = lax.ppermute(beyond, "lat", swap_next)

    arrays = (u_wind, v_wind, thickness, tracer, tables, damping)
    moved_bytes = sum(array.size * array.dtype.itemsize for array in arrays)
    send_shape = (sectors, 2 * lat_rows * level_rows, sector_wide)
    moved_shape = (lat_rows, 2 * level_rows, padded)
    held = (pltpu.HBM(u_wind.shape, bf16), pltpu.HBM(v_wind.shape, bf16), pltpu.VMEM(send_shape, bf16))
    in_held = [in_hbm, in_hbm, in_vmem]
    rows_shape = (3, lat_rows + 2, level_rows, lon_count)
    *loaded, u_filtered, v_filtered, send, moved, weights = pl.pallas_call(
        functools.partial(load, lat_count),
        out_shape=[pltpu.VMEM(array.shape, array.dtype) for array in arrays]
        + [*held, pltpu.VMEM(moved_shape, f32), pltpu.VMEM((3, level_count, sector_wide), f32)],
        in_specs=[in_hbm] * (2 + len(arrays)),
        out_specs=[in_vmem] * len(arrays) + in_held + [in_vmem] * 2,
        scratch_shapes=[
            pltpu.VMEM(rows_shape, f32),
            pltpu.VMEM((3, level_rows, padded), f32),
            pltpu.SMEM(remap_index.shape, jnp.int32),
            pltpu.SMEM(remap_frac.shape, f32),
            pltpu.SemaphoreType.DMA((9,)),
            pltpu.SemaphoreType.DMA((4,)),
        ],
        compiler_params=limit(8),
        cost_estimate=pl.CostEstimate(flops=0, bytes_accessed=moved_bytes, transcendentals=0),
        name="load",
    )(*(stay(array) for array in (remap_index, remap_frac, *arrays)))
    groups = 2 * lat_rows + 2
    before_held = len(loaded) + 3
    u_filtered, v_filtered, send = pl.pallas_call(
        functools.partial(filter_advect, lat_count),
        out_shape=held,
        in_specs=[in_vmem] * before_held + in_held,
        out_specs=tuple(in_held),
        input_output_aliases={before_held + i: i for i in range(3)},
        scratch_shapes=[
            pltpu.VMEM(u_wind.shape, bf16),
            pltpu.VMEM(v_wind.shape, bf16),
            pltpu.VMEM((groups, level_rows, padded), f32),
            pltpu.VMEM((groups, level_rows, padded), f32),
            pltpu.VMEM((2 * groups * level_rows, columns), bf16),
            pltpu.VMEM((2 * groups * level_rows, columns), f32),
            pltpu.VMEM((groups * level_rows, columns), bf16),
            pltpu.VMEM(rows_shape, f32),
            pltpu.VMEM(moved_shape, f32),
            pltpu.SemaphoreType.DMA((2,)),
        ],
        compiler_params=limit(20),
        name="filter_advect",
    )(*loaded, moved, near, beyond, u_filtered, v_filtered, send)
    recv = lax.all_to_all(send, "lev", split_axis=0, concat_axis=0, tiled=True)
    shape = (lat_rows, level_count, sector)
    thick_out, tracer_out = pl.pallas_call(
        remap,
        out_shape=(pltpu.HBM(shape, f32), pltpu.HBM(shape, f32)),
        in_specs=[in_vmem] * 2,
        out_specs=(in_hbm, in_hbm),
        scratch_shapes=[
            pltpu.VMEM(shape, f32),
            pltpu.VMEM(shape, f32),
            pltpu.SemaphoreType.DMA((2, lat_rows)),
        ],
        compiler_params=limit(8),
        name="remap",
    )(weights, recv)
    return u_filtered, v_filtered, thick_out, tracer_out


def solution(mesh):
    placed = (
        P("lat", "lev", None),
        P("lat", "lev", None),
        P("lat", "lev", None),
        P("lat", "lev", None),
        P(),
        P(),
    )
    return jax.shard_map(
        per_device,
        mesh=mesh,
        in_specs=placed,
        out_specs=(
            P("lat", "lev", None),
            P("lat", "lev", None),
            P("lat", None, "lev"),
            P("lat", None, "lev"),
        ),
        check_vma=False,
    )
```

time: 42.4 us -> 39.4 us (0.929)
  blocking collectives: 0 us -> 21.3 us
  waiting for transfers between devices: 14.3 us -> 0.82 us
  starting transfers between devices: 14.3 us -> 5.24 us
  Pallas kernels: 12.7 us -> 11.2 us
    all_to_all x0 -> x1, blocking collectives: none -> 21.3 us  [per_device(): recv = lax.all_to_all(send, 'lev', split_axis=0, concat_axis=0, tiled=True)]
    all_to_all x1 -> x0, waiting for transfers between devices: 13.2 us -> none  [per_device(): recv = lax.all_to_all(send, 'lev', split_axis=0, concat_axis=0, tiled=True)]
    all_to_all x1 -> x0, starting transfers between devices: 8.95 us -> none  [per_device(): recv = lax.all_to_all(send, 'lev', split_axis=0, concat_axis=0, tiled=True)]
    pallas_call x1, Pallas kernels: 6.92 us -> 5.33 us  [per_device(): pl.pallas_call(functools.partial(filter_advect, lat_count), out_shape=hel...]
  transfers between devices with their start and end apart: 3 -> 2, of which waited for: 2 -> 1; matrix products, arithmetic and copies ran while one was open for 0% -> 0% of each run, Pallas kernels for 8% -> 9%
where the time goes in v3:
time: 39.4 us; the launch traced here: 39.2 us
  blocking collectives  21.3 us (54%)
  Pallas kernels  11.2 us (28%)
  starting transfers between devices  5.24 us (13%)
  waiting for transfers between devices  0.82 us (2%)
  between operations  0.67 us (2%)
    all_to_all x1, blocking collectives, per_device(): recv = lax.all_to_all(send, 'lev', split_axis=0, concat_axis=0, tiled=True)  21.3 us
    pallas_call x1, Pallas kernels, per_device(): pl.pallas_call(functools.partial(filter_advect, lat_count), out_shape=hel...  5.33 us
    pallas_call x1, Pallas kernels, per_device(): pl.pallas_call(functools.partial(load, lat_count), out_shape=[pltpu.VMEM(...  3.63 us
    ppermute x1, starting transfers between devices, per_device(): near = lax.ppermute(near, 'lat', swap_near)  3.33 us
    ppermute x1, starting transfers between devices, per_device(): beyond = lax.ppermute(beyond, 'lat', swap_next)  1.91 us
    pallas_call x1, Pallas kernels, per_device(): pl.pallas_call(pack, out_shape=(pltpu.VMEM(edges, bf16), pltpu.VMEM(edges...  1.16 us
    pallas_call x1, Pallas kernels, per_device(): pl.pallas_call(remap, out_shape=(pltpu.HBM(shape, f32), pltpu.HBM(shape,...  1.05 us
    ppermute x1, waiting for transfers between devices, per_device(): beyond = lax.ppermute(beyond, 'lat', swap_next)  0.81 us
  transfers between devices with their start and end apart: 2, of which 1 were waited for; matrix products, arithmetic and copies ran while one was open for 0% of the time, Pallas kernels for 9%

profile of v3, /device:TPU:1, one launch (start us, length us, event | category | flops | bytes accessed | tf_op | source)
XLA Modules:
  0.0 39.2 jit_solution(18325254481858950612)
XLA Ops:
  0.6 1.2 %pack.1 = (bf16[3,8,2880]{2,1,0:T(8,128)(2,1)S(1)}, bf16[3,8,2880]{2,1,0:T(8,128)(2,1)S(1)}) custom-call(bf16[4,8,2880]{2,1,0:T(8,128)(2,1)} %v_hbm.3, f32[4,8,2880]{2,1,0:T(8,128)} %thick_hbm.3, f32[4,8,2880]{2,1,0:T(8,128)} %tracer_hbm.3), custom_call_target="tpu_custom_call" | custom-call | tf_op jit(solution)/shard_map/pack/pallas_call | solution.py:563
  1.8 3.3 %collective-permute-start = (bf16[3,8,2880]{2,1,0:T(8,128)(2,1)S(1)}, bf16[3,8,2880]{2,1,0:T(8,128)(2,1)S(1)}, u32[]{:S(2)}, u32[]{:S(2)}) collective-permute-start(bf16[3,8,2880]{2,1,0:T(8,128)(2,1)S(1)} %get-tuple-element.29), channel_id=1, source_target_pairs={{0,8},{8,0},{16,24},{24,16},{32,40},{40,32},{48,56},{56,48},{64,72... | collective-permute-start | bytes 414728 | tf_op jit(solution)/shard_map/ppermute | solution.py:579
  5.1 1.9 %collective-permute-start.1 = (bf16[3,8,2880]{2,1,0:T(8,128)(2,1)S(1)}, bf16[3,8,2880]{2,1,0:T(8,128)(2,1)S(1)}, u32[]{:S(2)}, u32[]{:S(2)}) collective-permute-start(bf16[3,8,2880]{2,1,0:T(8,128)(2,1)S(1)} %get-tuple-element.30), channel_id=1, source_target_pairs={{8,16},{16,8},{24,32},{32,24},{40,48},{48,40},{56,64},{64,56},{72,... | collective-permute-start | bytes 414728 | tf_op jit(solution)/shard_map/ppermute | solution.py:580
  7.0 3.6 %load.1 = (bf16[4,8,2880]{2,1,0:T(8,128)(2,1)S(1)}, bf16[4,8,2880]{2,1,0:T(8,128)(2,1)S(1)}, f32[4,8,2880]{2,1,0:T(8,128)S(1)}, f32[4,8,2880]{2,1,0:T(8,128)S(1)...) custom-call(s32[65]{0:T(128)} %index_hbm.1, ...), custom_call_target="tpu_custom_call" | custom-call | bytes 8392704 | tf_op jit(solution)/shard_map/load/pallas_call | solution.py:589
  10.7 0.0 collective-permute-done.near_ref
  10.7 0.8 %collective-permute-done.1.next_ref = bf16[3,8,2880]{2,1,0:T(8,128)(2,1)S(1)} collective-permute-done((bf16[3,8,2880]{2,1,0:T(8,128)(2,1)S(1)}, bf16[3,8,2880]{2,1,0:T(8,128)(2,1)S(1)}, u32[]{:S(2)}, u32[]{:S(2)}) %collective-permute-start.1) | collective-permute-done | bytes 138272 | tf_op jit(solution)/shard_map/ppermute | solution.py:580
  11.5 5.3 %filter_advect.1 = (bf16[4,8,2880]{2,1,0:T(8,128)(2,1)}, bf16[4,8,2880]{2,1,0:T(8,128)(2,1)}, bf16[8,64,384]{2,1,0:T(8,128)(2,1)S(1)}) custom-call(bf16[4,8,2880]{2,1,0:T(8,128)(2,1)S(1)} %get-tuple-element.22.u_ref, bf16[4,8,2880]{2,1,0:T(8,128)(2,1)S(1)} %get-tuple-element.23.v_ref, ...), custom_call_target="tpu_custom_call", output_to_operand_aliasing={{0}: (9, {}), {1}: (10, {}), {2}: (11, {})} | custom-call | tf_op jit(solution)/shard_map/filter_advect/pallas_call | solution.py:609
  16.9 21.3 %all_to_all.5.recv_ref = bf16[8,64,384]{2,1,0:T(8,128)(2,1)S(1)} all-to-all(bf16[8,64,384]{2,1,0:T(8,128)(2,1)S(1)} %get-tuple-element.37), channel_id=1, replica_groups=mesh['lat'=32,'lev'=8] {'lev'}, dimensions={0} | all-to-all | bytes 786432 | tf_op jit(solution)/shard_map/all_to_all | solution.py:630
  38.1 1.0 %remap.1 = (f32[4,64,360]{2,1,0:T(8,128)}, f32[4,64,360]{2,1,0:T(8,128)}) custom-call(f32[3,64,384]{2,1,0:T(8,128)S(1)} %get-tuple-element.36.weight_ref, bf16[8,64,384]{2,1,0:T(8,128)(2,1)S(1)} %all_to_all.5.recv_ref), custom_call_target="tpu_custom_call" | custom-call | tf_op jit(solution)/shard_map/remap/pallas_call | solution.py:632
Async XLA Ops:
  1.8 8.9 %collective-permute-start = (bf16[3,8,2880]{2,1,0:T(8,128)(2,1)S(1)}, bf16[3,8,2880]{2,1,0:T(8,128)(2,1)S(1)}, u32[]{:S(2)}, u32[]{:S(2)}) collective-permute-start(bf16[3,8,2880]{2,1,0:T(8,128)(2,1)S(1)} %get-tuple-element.29), channel_id=1, source_target_pairs={{0,8},{8,0},{16,24},{24,16},{32,40},{40,32},{48,56},{56,48},{64,72... | collective-permute-start | bytes 414728 | tf_op jit(solution)/shard_map/ppermute | solution.py:579
  5.1 6.4 %collective-permute-start.1 = (bf16[3,8,2880]{2,1,0:T(8,128)(2,1)S(1)}, bf16[3,8,2880]{2,1,0:T(8,128)(2,1)S(1)}, u32[]{:S(2)}, u32[]{:S(2)}) collective-permute-start(bf16[3,8,2880]{2,1,0:T(8,128)(2,1)S(1)} %get-tuple-element.30), channel_id=1, source_target_pairs={{8,16},{16,8},{24,32},{32,24},{40,48},{48,40},{56,64},{64,56},{72,... | collective-permute-start | bytes 414728 | tf_op jit(solution)/shard_map/ppermute | solution.py:580

commit v4 on v3

--- a/solution.py
+++ b/solution.py
@@ -100,12 +100,12 @@
     return jnp.clip(0.05 * wind, -0.15, 0.15)
 
 
-def loop(count, body):
+def loop(count, body, unroll=1):
     def step(place, carry):
         body(place)
         return carry
 
-    lax.fori_loop(0, count, step, 0)
+    lax.fori_loop(0, count, step, 0, unroll=unroll)
 
 
 def rows_at(place, count):
@@ -155,11 +155,11 @@
         return up_and_down(face * jnp.where(inside, 1.0, 0.0))
 
     (rise_below, fall_below), (rise_above, fall_above) = face_y(j), face_y(j + 1)
-    courant_x = extend(0, courant(wind_ref[j].astype(jnp.float32)))
+    courant_x = extend(3 * (j % 2), courant(wind_ref[j].astype(jnp.float32)))
     rise_x, fall_x = up_and_down(0.5 * (before(courant_x) + courant_x))
     for i in range(2):
         below, here, above = (row_ref[1 + i, j + k] for k in range(3))
-        field = extend(1 + i, here)
+        field = extend(3 * (j % 2) + 1 + i, here)
         flux_x = rise_x * before(field) + fall_x * field
         across = rise_above * here + fall_above * above - rise_below * below - fall_below * here
         result = field - (after(flux_x) - flux_x)
@@ -186,6 +186,30 @@
             weight_ref[place, pl.ds(k, 1), :] = jnp.full((1, wide), weight, jnp.float32)
 
     loop(level_count, weigh)
+
+
+def fold(wind, slot, slot_ref, work_ref, split_ref, rows):
+    level_rows, lon_count = wind.shape
+    padded = slot_ref.shape[2]
+    parts, _ = filter_parts(lon_count)
+    half, quarter, eighth = (part[2] for part in parts[:3])
+    half_wide, quarter_wide, eighth_wide = (padded_to(part[2]) for part in parts[:3])
+    slot_ref[slot, :, lon_count:] = jnp.zeros((level_rows, padded - lon_count), jnp.float32)
+    slot_ref[slot, :, :lon_count] = wind
+    near = slot_ref[slot, :, :half_wide]
+    far = slot_ref[slot, :, half : half + half_wide]
+    odd, even = near - far, near + far
+    work_ref[slot, :, :half_wide] = even
+    near = even[:, :quarter_wide]
+    far = work_ref[slot, :, quarter : quarter + quarter_wide]
+    two, even = near - far, near + far
+    work_ref[slot, :, half_wide : half_wide + quarter_wide] = even
+    near = even[:, :eighth_wide]
+    far = work_ref[slot, :, half_wide + eighth : half_wide + eighth + eighth_wide]
+    row = jnp.concatenate([odd, two, near - far, near + far], axis=1)
+    high = row.astype(jnp.bfloat16).astype(jnp.float32)
+    both = jnp.concatenate([high, row - high], axis=0)
+    split_ref[rows, :] = both.astype(jnp.bfloat16)
 
 
 def load(
@@ -204,13 +228,16 @@
     tracer_ref,
     table_ref,
     damp_ref,
+    turned_ref,
     u_out,
     v_out,
     send_ref,
+    split_ref,
     moved_ref,
     weight_ref,
     row_ref,
     real_ref,
+    work_ref,
     index_ref,
     frac_ref,
     sems,
@@ -226,13 +253,23 @@
         )
     ]
     tables = [pltpu.make_async_copy(damp_hbm, damp_ref, sems.at[4])]
-    chunks = table_sems.shape[0]
-    height = table_hbm.shape[0] // chunks
-    for chunk in range(chunks):
-        part = pl.ds(chunk * height, height)
-        tables.append(
-            pltpu.make_async_copy(table_hbm.at[part], table_ref.at[part], table_sems.at[chunk])
+    parts, _ = filter_parts(lon_count)
+    places = table_places(parts)
+    points, split_at, columns = parts[0][2], places[0][2], table_hbm.shape[1]
+    upper = places[2][0] + places[2][2]
+    chunks = table_sems.shape[0] - 1
+    height = upper // chunks
+
+    def table_copy(chunk):
+        if isinstance(chunk, int) and chunk == chunks:
+            part = (pl.ds(upper, points - upper), pl.ds(0, split_at))
+        else:
+            part = (rows_at(chunk, height), pl.ds(0, columns))
+        return pltpu.make_async_copy(
+            table_hbm.at[part], table_ref.at[part], table_sems.at[chunk]
         )
+
+    tables += [table_copy(chunk) for chunk in range(chunks + 1)]
     for copy in inputs:
         copy.start()
 
@@ -258,8 +295,22 @@
         weigh()
         for copy in inputs:
             copy.wait()
-        for copy in tables:
-            copy.wait()
+        slots = real_ref.shape[0]
+        for g in range(2 * lat_rows):
+            wind = (u_ref if g < lat_rows else v_ref)[g % lat_rows].astype(f32)
+            rows = slice(2 * level_rows * g, 2 * level_rows * (g + 1))
+            fold(wind, g % slots, real_ref, work_ref, split_ref, rows)
+        table_ref[points:split_at, :split_at] = jnp.zeros((split_at - points, split_at), jnp.bfloat16)
+        for chunk in range(chunks + 1):
+            table_copy(chunk).wait()
+            start, stop = chunk * height, (chunk + 1) * height
+            for top, left, size in places:
+                low, high = max(start, top), min(stop, top + size)
+                if low < high:
+                    turned_ref[top : top + size, left + low - top : left + high - top] = (
+                        table_ref[low:high, left : left + size].T
+                    )
+        tables[0].wait()
 
     @pl.when(jnp.logical_not(polar))
     def _():
@@ -291,7 +342,7 @@
             def _():
                 to_sectors(send_ref, moved_ref, j, lon_count // send_ref.shape[0])
 
-        loop(lat_rows, advect)
+        loop(lat_rows, advect, 2)
         weigh()
         for copy in winds:
             copy.wait()
@@ -305,20 +356,22 @@
     tracer_ref,
     table_ref,
     damp_ref,
+    turned_ref,
     partial_ref,
+    next_ref,
     near_ref,
-    next_ref,
     u_held,
     v_held,
     send_held,
+    split_held,
     u_hbm,
     v_hbm,
     send_ref,
+    split_ref,
     u_out,
     v_out,
     real_ref,
     work_ref,
-    split_ref,
     prod_ref,
     spec_ref,
     row_ref,
@@ -377,35 +430,19 @@
             v_out[j] = v_ref[j]
 
         loop(lat_rows, prepare)
-        half, quarter, eighth = parts[0][2], parts[1][2], parts[2][2]
+        half, quarter, eighth = (part[2] for part in parts[:3])
         half_wide, quarter_wide, eighth_wide = (padded_to(part[2]) for part in parts[:3])
-        last = lat_rows + 2
 
         def lat_of(g):
-            return first_lat + (g if g < lat_rows else g - lat_rows - 1)
-
-        def fold(g, wind):
-            real_ref[g, :, lon_count:] = jnp.zeros((level_rows, padded - lon_count), f32)
-            real_ref[g, :, :lon_count] = wind
-            near = real_ref[g, :, :half_wide]
-            far = real_ref[g, :, half : half + half_wide]
-            odd, even = near - far, near + far
-            work_ref[g, :, :half_wide] = even
-            near = even[:, :quarter_wide]
-            far = work_ref[g, :, quarter : quarter + quarter_wide]
-            two, even = near - far, near + far
-            work_ref[g, :, half_wide : half_wide + quarter_wide] = even
-            near = even[:, :eighth_wide]
-            far = work_ref[g, :, half_wide + eighth : half_wide + eighth + eighth_wide]
-            row = jnp.concatenate([odd, two, near - far, near + far], axis=1)
-            high = row.astype(bf16).astype(f32)
-            both = jnp.concatenate([high, row - high], axis=0)
-            split_ref[rows_at(g, 2 * level_rows), :] = both.astype(bf16)
-
-        for j in range(lat_rows):
-            fold(j, u_ref[j].astype(f32))
-        for j in range(last):
-            fold(lat_rows + j, row_ref[0, j])
+            if g < 2 * lat_rows:
+                return first_lat + g % lat_rows
+            return first_lat + (lat_rows if g % 2 else -1)
+
+        for side in range(2):
+            g = 2 * lat_rows + side
+            rows = slice(2 * level_rows * g, 2 * level_rows * (g + 1))
+            wind = row_ref[0, side * (lat_rows + 1)]
+            fold(wind, side, real_ref, work_ref, split_ref, rows)
 
         for (_, _, _, column), (top, left, size) in zip(parts, places):
             prod_ref[:, column : column + size] = jnp.dot(
@@ -428,10 +465,9 @@
         rows = groups * level_rows
 
         for (_, _, _, column), (top, left, size) in zip(parts, places):
-            prod_ref[:rows, column : column + size] = lax.dot_general(
+            prod_ref[:rows, column : column + size] = jnp.dot(
                 spec_ref[:, column : column + size],
-                table_ref[top : top + size, left : left + size],
-                (((1,), (1,)), ((), ())),
+                turned_ref[top : top + size, left : left + size],
                 preferred_element_type=f32,
             )
 
@@ -452,19 +488,20 @@
             real_ref[g, :, half : 2 * half] = ((even - odd) * scale)[:, :half]
 
         def finish(j):
-            smooth = real_ref[lat_rows + j, :, :lon_count].astype(bf16)
-
-            @pl.when(is_polar(first_lat + j - 1, lat_count))
+            @pl.when(is_polar(first_lat + j, lat_count))
             def _():
-                row_ref[0, j] = smooth.astype(f32)
-
-                @pl.when(jnp.logical_and(j > 0, j <= lat_rows))
-                def _():
-                    inner = jnp.clip(j - 1, 0, lat_rows - 1)
-                    v_out[inner] = smooth
-                    u_out[inner] = real_ref[inner, :, :lon_count].astype(bf16)
-
-        loop(last, finish)
+                u_out[j] = real_ref[j, :, :lon_count].astype(bf16)
+                smooth = real_ref[lat_rows + j, :, :lon_count].astype(bf16)
+                v_out[j] = smooth
+                row_ref[0, j + 1] = smooth.astype(f32)
+
+        loop(lat_rows, finish)
+        for side in range(2):
+
+            @pl.when(is_polar(lat_of(2 * lat_rows + side), lat_count))
+            def _():
+                smooth = real_ref[2 * lat_rows + side, :, :lon_count].astype(bf16)
+                row_ref[0, side * (lat_rows + 1)] = smooth.astype(f32)
 
         winds_out = [
             pltpu.make_async_copy(u_out, u_hbm, sems.at[0]),
@@ -479,7 +516,7 @@
             transport(j, u_out, row_ref, real_ref, moved_ref, least, most)
             to_sectors(send_ref, moved_ref, j, lon_count // send_ref.shape[0])
 
-        loop(lat_rows, advect)
+        loop(lat_rows, advect, 2)
         for copy in winds_out:
             copy.wait()
 
@@ -583,18 +620,25 @@
     moved_bytes = sum(array.size * array.dtype.itemsize for array in arrays)
     send_shape = (sectors, 2 * lat_rows * level_rows, sector_wide)
     moved_shape = (lat_rows, 2 * level_rows, padded)
-    held = (pltpu.HBM(u_wind.shape, bf16), pltpu.HBM(v_wind.shape, bf16), pltpu.VMEM(send_shape, bf16))
-    in_held = [in_hbm, in_hbm, in_vmem]
+    groups = 2 * lat_rows + 2
+    held = (
+        pltpu.HBM(u_wind.shape, bf16),
+        pltpu.HBM(v_wind.shape, bf16),
+        pltpu.VMEM(send_shape, bf16),
+        pltpu.VMEM((2 * groups * level_rows, columns), bf16),
+    )
+    in_held = [in_hbm, in_hbm, in_vmem, in_vmem]
     rows_shape = (3, lat_rows + 2, level_rows, lon_count)
-    *loaded, u_filtered, v_filtered, send, moved, weights = pl.pallas_call(
+    *loaded, u_filtered, v_filtered, send, split, moved, weights = pl.pallas_call(
         functools.partial(load, lat_count),
-        out_shape=[pltpu.VMEM(array.shape, array.dtype) for array in arrays]
+        out_shape=[pltpu.VMEM(array.shape, array.dtype) for array in (*arrays, tables)]
         + [*held, pltpu.VMEM(moved_shape, f32), pltpu.VMEM((3, level_count, sector_wide), f32)],
         in_specs=[in_hbm] * (2 + len(arrays)),
-        out_specs=[in_vmem] * len(arrays) + in_held + [in_vmem] * 2,
+        out_specs=[in_vmem] * (len(arrays) + 1) + in_held + [in_vmem] * 2,
         scratch_shapes=[
             pltpu.VMEM(rows_shape, f32),
-            pltpu.VMEM((3, level_rows, padded), f32),
+            pltpu.VMEM((6, level_rows, padded), f32),
+            pltpu.VMEM((6, level_rows, padded), f32),
             pltpu.SMEM(remap_index.shape, jnp.int32),
             pltpu.SMEM(remap_frac.shape, f32),
             pltpu.SemaphoreType.DMA((9,)),
@@ -604,20 +648,18 @@
         cost_estimate=pl.CostEstimate(flops=0, bytes_accessed=moved_bytes, transcendentals=0),
         name="load",
     )(*(stay(array) for array in (remap_index, remap_frac, *arrays)))
-    groups = 2 * lat_rows + 2
     before_held = len(loaded) + 3
-    u_filtered, v_filtered, send = pl.pallas_call(
+    u_filtered, v_filtered, send, _ = pl.pallas_call(
         functools.partial(filter_advect, lat_count),
         out_shape=held,
         in_specs=[in_vmem] * before_held + in_held,
         out_specs=tuple(in_held),
-        input_output_aliases={before_held + i: i for i in range(3)},
+        input_output_aliases={before_held + i: i for i in range(4)},
         scratch_shapes=[
             pltpu.VMEM(u_wind.shape, bf16),
             pltpu.VMEM(v_wind.shape, bf16),
             pltpu.VMEM((groups, level_rows, padded), f32),
             pltpu.VMEM((groups, level_rows, padded), f32),
-            pltpu.VMEM((2 * groups * level_rows, columns), bf16),
             pltpu.VMEM((2 * groups * level_rows, columns), f32),
             pltpu.VMEM((groups * level_rows, columns), bf16),
             pltpu.VMEM(rows_shape, f32),
@@ -626,7 +668,7 @@
         ],
         compiler_params=limit(20),
         name="filter_advect",
-    )(*loaded, moved, near, beyond, u_filtered, v_filtered, send)
+    )(*loaded, moved, beyond, near, u_filtered, v_filtered, send, split)
     recv = lax.all_to_all(send, "lev", split_axis=0, concat_axis=0, tiled=True)
     shape = (lat_rows, level_count, sector)
     thick_out, tracer_out = pl.pallas_call(

time: 39.4 us -> 39.2 us (level)
  blocking collectives: 21.3 us -> 22.7 us
  waiting for transfers between devices: 0.82 us -> 0.01 us
  Pallas kernels: 11.2 us -> 10.6 us
  starting transfers between devices: 5.24 us -> 4.69 us
    ppermute x1, starting transfers between devices: 3.33 us -> 0.09 us  [per_device(): near = lax.ppermute(near, 'lat', swap_near)]
    ppermute x1, starting transfers between devices: 1.91 us -> 4.59 us  [per_device(): beyond = lax.ppermute(beyond, 'lat', swap_next)]
    all_to_all x1, blocking collectives: 21.3 us -> 22.7 us  [per_device(): recv = lax.all_to_all(send, 'lev', split_axis=0, concat_axis=0, tiled=True)]
    pallas_call x1, Pallas kernels: 5.33 us -> 4.33 us  [per_device(): pl.pallas_call(functools.partial(filter_advect, lat_count), out_shape=hel...]
    ppermute x1, waiting for transfers between devices: 0.81 us -> 0.01 us  [per_device(): beyond = lax.ppermute(beyond, 'lat', swap_next)]
  transfers between devices with their start and end apart: 2 -> 2, of which waited for: 1 -> 0; matrix products, arithmetic and copies ran while one was open for 0% -> 0% of each run, Pallas kernels for 9% -> 10%
where the time goes in v4:
time: 39.2 us; the launch traced here: 38.6 us
  blocking collectives  22.7 us (58%)
  Pallas kernels  10.6 us (27%)
  starting transfers between devices  4.69 us (12%)
  between operations  0.69 us (2%)
    all_to_all x1, blocking collectives, per_device(): recv = lax.all_to_all(send, 'lev', split_axis=0, concat_axis=0, tiled=True)  22.7 us
    ppermute x1, starting transfers between devices, per_device(): beyond = lax.ppermute(beyond, 'lat', swap_next)  4.59 us
    pallas_call x1, Pallas kernels, per_device(): pl.pallas_call(functools.partial(filter_advect, lat_count), out_shape=hel...  4.33 us
    pallas_call x1, Pallas kernels, per_device(): pl.pallas_call(functools.partial(load, lat_count), out_shape=[pltpu.VMEM(...  4.01 us
    pallas_call x1, Pallas kernels, per_device(): pl.pallas_call(pack, out_shape=(pltpu.VMEM(edges, bf16), pltpu.VMEM(edges...  1.16 us
    pallas_call x1, Pallas kernels, per_device(): pl.pallas_call(remap, out_shape=(pltpu.HBM(shape, f32), pltpu.HBM(shape,...  1.05 us
  transfers between devices with their start and end apart: 2, of which 0 were waited for; matrix products, arithmetic and copies ran while one was open for 0% of the time, Pallas kernels for 10%

profile of v4, /device:TPU:1, one launch (start us, length us, event | category | flops | bytes accessed | tf_op | source)
XLA Modules:
  0.0 38.6 jit_solution(13500631132181202943)
XLA Ops:
  0.6 1.2 %pack.1 = (bf16[3,8,2880]{2,1,0:T(8,128)(2,1)S(1)}, bf16[3,8,2880]{2,1,0:T(8,128)(2,1)S(1)}) custom-call(bf16[4,8,2880]{2,1,0:T(8,128)(2,1)} %v_hbm.3, f32[4,8,2880]{2,1,0:T(8,128)} %thick_hbm.3, f32[4,8,2880]{2,1,0:T(8,128)} %tracer_hbm.3), custom_call_target="tpu_custom_call" | custom-call | tf_op jit(solution)/shard_map/pack/pallas_call | solution.py:600
  1.8 4.6 %collective-permute-start = (bf16[3,8,2880]{2,1,0:T(8,128)(2,1)S(1)}, bf16[3,8,2880]{2,1,0:T(8,128)(2,1)S(1)}, u32[]{:S(2)}, u32[]{:S(2)}) collective-permute-start(bf16[3,8,2880]{2,1,0:T(8,128)(2,1)S(1)} %get-tuple-element.32), channel_id=1, source_target_pairs={{8,16},{16,8},{24,32},{32,24},{40,48},{48,40},{56,64},{64,56},{72,... | collective-permute-start | bytes 414728 | tf_op jit(solution)/shard_map/ppermute | solution.py:617
  6.4 0.1 collective-permute-start.1
  6.5 4.0 %load.1 = (bf16[4,8,2880]{2,1,0:T(8,128)(2,1)S(1)}, bf16[4,8,2880]{2,1,0:T(8,128)(2,1)S(1)}, f32[4,8,2880]{2,1,0:T(8,128)S(1)}, f32[4,8,2880]{2,1,0:T(8,128)S(1)...) custom-call(s32[65]{0:T(128)} %index_hbm.1, ...), custom_call_target="tpu_custom_call" | custom-call | bytes 8392704 | tf_op jit(solution)/shard_map/load/pallas_call | solution.py:632
  10.5 0.0 collective-permute-done.next_ref
  10.5 0.0 collective-permute-done.1.near_ref
  10.5 4.3 %filter_advect.1 = (bf16[4,8,2880]{2,1,0:T(8,128)(2,1)}, bf16[4,8,2880]{2,1,0:T(8,128)(2,1)}, bf16[8,64,384]{2,1,0:T(8,128)(2,1)S(1)}, bf16[160,3072]{1,0:T(8,128)(2,1)S(1)}) custom-call(bf16[4,8,2880]{2,1,0:T(8,128)(2,1)S(1)} %get-tuple-element.24.u_ref, ...), custom_call_target="tpu_custom_call", output_to_operand_aliasing={{0}: (10, {}), {1}: (11, {}), {2}: (12, {}), {3}: (13, {})} | custom-call | tf_op jit(solution)/shard_map/filter_advect/pallas_call | solution.py:652
  14.9 22.7 %all_to_all.5.recv_ref = bf16[8,64,384]{2,1,0:T(8,128)(2,1)S(1)} all-to-all(bf16[8,64,384]{2,1,0:T(8,128)(2,1)S(1)} %get-tuple-element.41), channel_id=1, replica_groups=mesh['lat'=32,'lev'=8] {'lev'}, dimensions={0} | all-to-all | bytes 786432 | tf_op jit(solution)/shard_map/all_to_all | solution.py:672
  37.6 1.0 %remap.1 = (f32[4,64,360]{2,1,0:T(8,128)}, f32[4,64,360]{2,1,0:T(8,128)}) custom-call(f32[3,64,384]{2,1,0:T(8,128)S(1)} %get-tuple-element.40.weight_ref, bf16[8,64,384]{2,1,0:T(8,128)(2,1)S(1)} %all_to_all.5.recv_ref), custom_call_target="tpu_custom_call" | custom-call | tf_op jit(solution)/shard_map/remap/pallas_call | solution.py:674
Async XLA Ops:
  1.8 8.7 %collective-permute-start = (bf16[3,8,2880]{2,1,0:T(8,128)(2,1)S(1)}, bf16[3,8,2880]{2,1,0:T(8,128)(2,1)S(1)}, u32[]{:S(2)}, u32[]{:S(2)}) collective-permute-start(bf16[3,8,2880]{2,1,0:T(8,128)(2,1)S(1)} %get-tuple-element.32), channel_id=1, source_target_pairs={{8,16},{16,8},{24,32},{32,24},{40,48},{48,40},{56,64},{64,56},{72,... | collective-permute-start | bytes 414728 | tf_op jit(solution)/shard_map/ppermute | solution.py:617
  6.4 4.1 %collective-permute-start.1 = (bf16[3,8,2880]{2,1,0:T(8,128)(2,1)S(1)}, bf16[3,8,2880]{2,1,0:T(8,128)(2,1)S(1)}, u32[]{:S(2)}, u32[]{:S(2)}) collective-permute-start(bf16[3,8,2880]{2,1,0:T(8,128)(2,1)S(1)} %get-tuple-element.33), channel_id=1, source_target_pairs={{0,8},{8,0},{16,24},{24,16},{32,40},{40,32},{48,56},{56,48},{64,72... | collective-permute-start | bytes 414728 | tf_op jit(solution)/shard_map/ppermute | solution.py:616

commit v5 on v4

--- a/solution.py
+++ b/solution.py
@@ -12,7 +12,7 @@
 
 COS_EDGE = math.cos(66.0 * math.pi / 180.0)
 LANES = 128
-THICK_MID = 1.25
+THICK_MID = 1.0
 
 
 def padded_to(count):

time: 39.2 us -> 39.2 us (level)
  no operation moved by 1% of the time
where the time goes in v5:
time: 39.2 us; the launch traced here: 38.6 us
  blocking collectives  22.7 us (58%)
  Pallas kernels  10.6 us (27%)
  starting transfers between devices  4.69 us (12%)
  between operations  0.69 us (2%)
    all_to_all x1, blocking collectives, per_device(): recv = lax.all_to_all(send, 'lev', split_axis=0, concat_axis=0, tiled=True)  22.7 us
    ppermute x1, starting transfers between devices, per_device(): beyond = lax.ppermute(beyond, 'lat', swap_next)  4.59 us
    pallas_call x1, Pallas kernels, per_device(): pl.pallas_call(functools.partial(filter_advect, lat_count), out_shape=hel...  4.33 us
    pallas_call x1, Pallas kernels, per_device(): pl.pallas_call(functools.partial(load, lat_count), out_shape=[pltpu.VMEM(...  4.01 us
    pallas_call x1, Pallas kernels, per_device(): pl.pallas_call(pack, out_shape=(pltpu.VMEM(edges, bf16), pltpu.VMEM(edges...  1.16 us
    pallas_call x1, Pallas kernels, per_device(): pl.pallas_call(remap, out_shape=(pltpu.HBM(shape, f32), pltpu.HBM(shape,...  1.05 us
  transfers between devices with their start and end apart: 2, of which 0 were waited for; matrix products, arithmetic and copies ran while one was open for 0% of the time, Pallas kernels for 10%

profile of v5, /device:TPU:1, one launch (start us, length us, event | category | flops | bytes accessed | tf_op | source)
XLA Modules:
  0.0 38.6 jit_solution(2436767467194773882)
XLA Ops:
  0.6 1.2 %pack.1 = (bf16[3,8,2880]{2,1,0:T(8,128)(2,1)S(1)}, bf16[3,8,2880]{2,1,0:T(8,128)(2,1)S(1)}) custom-call(bf16[4,8,2880]{2,1,0:T(8,128)(2,1)} %v_hbm.3, f32[4,8,2880]{2,1,0:T(8,128)} %thick_hbm.3, f32[4,8,2880]{2,1,0:T(8,128)} %tracer_hbm.3), custom_call_target="tpu_custom_call" | custom-call | tf_op jit(solution)/shard_map/pack/pallas_call | solution.py:600
  1.8 4.6 %collective-permute-start = (bf16[3,8,2880]{2,1,0:T(8,128)(2,1)S(1)}, bf16[3,8,2880]{2,1,0:T(8,128)(2,1)S(1)}, u32[]{:S(2)}, u32[]{:S(2)}) collective-permute-start(bf16[3,8,2880]{2,1,0:T(8,128)(2,1)S(1)} %get-tuple-element.32), channel_id=1, source_target_pairs={{8,16},{16,8},{24,32},{32,24},{40,48},{48,40},{56,64},{64,56},{72,... | collective-permute-start | bytes 414728 | tf_op jit(solution)/shard_map/ppermute | solution.py:617
  6.4 0.1 collective-permute-start.1
  6.5 4.0 %load.1 = (bf16[4,8,2880]{2,1,0:T(8,128)(2,1)S(1)}, bf16[4,8,2880]{2,1,0:T(8,128)(2,1)S(1)}, f32[4,8,2880]{2,1,0:T(8,128)S(1)}, f32[4,8,2880]{2,1,0:T(8,128)S(1)...) custom-call(s32[65]{0:T(128)} %index_hbm.1, ...), custom_call_target="tpu_custom_call" | custom-call | bytes 8392704 | tf_op jit(solution)/shard_map/load/pallas_call | solution.py:632
  10.5 0.0 collective-permute-done.next_ref
  10.5 0.0 collective-permute-done.1.near_ref
  10.5 4.3 %filter_advect.1 = (bf16[4,8,2880]{2,1,0:T(8,128)(2,1)}, bf16[4,8,2880]{2,1,0:T(8,128)(2,1)}, bf16[8,64,384]{2,1,0:T(8,128)(2,1)S(1)}, bf16[160,3072]{1,0:T(8,128)(2,1)S(1)}) custom-call(bf16[4,8,2880]{2,1,0:T(8,128)(2,1)S(1)} %get-tuple-element.24.u_ref, ...), custom_call_target="tpu_custom_call", output_to_operand_aliasing={{0}: (10, {}), {1}: (11, {}), {2}: (12, {}), {3}: (13, {})} | custom-call | tf_op jit(solution)/shard_map/filter_advect/pallas_call | solution.py:652
  14.9 22.7 %all_to_all.5.recv_ref = bf16[8,64,384]{2,1,0:T(8,128)(2,1)S(1)} all-to-all(bf16[8,64,384]{2,1,0:T(8,128)(2,1)S(1)} %get-tuple-element.41), channel_id=1, replica_groups=mesh['lat'=32,'lev'=8] {'lev'}, dimensions={0} | all-to-all | bytes 786432 | tf_op jit(solution)/shard_map/all_to_all | solution.py:672
  37.6 1.0 %remap.1 = (f32[4,64,360]{2,1,0:T(8,128)}, f32[4,64,360]{2,1,0:T(8,128)}) custom-call(f32[3,64,384]{2,1,0:T(8,128)S(1)} %get-tuple-element.40.weight_ref, bf16[8,64,384]{2,1,0:T(8,128)(2,1)S(1)} %all_to_all.5.recv_ref), custom_call_target="tpu_custom_call" | custom-call | tf_op jit(solution)/shard_map/remap/pallas_call | solution.py:674
Async XLA Ops:
  1.8 8.7 %collective-permute-start = (bf16[3,8,2880]{2,1,0:T(8,128)(2,1)S(1)}, bf16[3,8,2880]{2,1,0:T(8,128)(2,1)S(1)}, u32[]{:S(2)}, u32[]{:S(2)}) collective-permute-start(bf16[3,8,2880]{2,1,0:T(8,128)(2,1)S(1)} %get-tuple-element.32), channel_id=1, source_target_pairs={{8,16},{16,8},{24,32},{32,24},{40,48},{48,40},{56,64},{64,56},{72,... | collective-permute-start | bytes 414728 | tf_op jit(solution)/shard_map/ppermute | solution.py:617
  6.4 4.1 %collective-permute-start.1 = (bf16[3,8,2880]{2,1,0:T(8,128)(2,1)S(1)}, bf16[3,8,2880]{2,1,0:T(8,128)(2,1)S(1)}, u32[]{:S(2)}, u32[]{:S(2)}) collective-permute-start(bf16[3,8,2880]{2,1,0:T(8,128)(2,1)S(1)} %get-tuple-element.33), channel_id=1, source_target_pairs={{0,8},{8,0},{16,24},{24,16},{32,40},{40,32},{48,56},{56,48},{64,72... | collective-permute-start | bytes 414728 | tf_op jit(solution)/shard_map/ppermute | solution.py:616

commit v6 on v5

--- a/solution.py
+++ b/solution.py
@@ -314,6 +314,7 @@
 
     @pl.when(jnp.logical_not(polar))
     def _():
+        weigh()
         for copy in inputs:
             copy.wait()
         winds = [
@@ -343,7 +344,6 @@
                 to_sectors(send_ref, moved_ref, j, lon_count // send_ref.shape[0])
 
         loop(lat_rows, advect, 2)
-        weigh()
         for copy in winds:
             copy.wait()
 

time: 39.2 us -> 38.8 us (0.990)
  blocking collectives: 22.7 us -> 22.3 us
    all_to_all x1, blocking collectives: 22.7 us -> 22.3 us  [per_device(): recv = lax.all_to_all(send, 'lev', split_axis=0, concat_axis=0, tiled=True)]
  transfers between devices with their start and end apart: 2 -> 2, of which waited for: 0 -> 0; matrix products, arithmetic and copies ran while one was open for 0% -> 0% of each run, Pallas kernels for 10% -> 11%
where the time goes in v6:
time: 38.8 us; the launch traced here: 38.2 us
  blocking collectives  22.3 us (57%)
  Pallas kernels  10.6 us (27%)
  starting transfers between devices  4.69 us (12%)
  between operations  0.69 us (2%)
    all_to_all x1, blocking collectives, per_device(): recv = lax.all_to_all(send, 'lev', split_axis=0, concat_axis=0, tiled=True)  22.3 us
    ppermute x1, starting transfers between devices, per_device(): beyond = lax.ppermute(beyond, 'lat', swap_next)  4.59 us
    pallas_call x1, Pallas kernels, per_device(): pl.pallas_call(functools.partial(filter_advect, lat_count), out_shape=hel...  4.33 us
    pallas_call x1, Pallas kernels, per_device(): pl.pallas_call(functools.partial(load, lat_count), out_shape=[pltpu.VMEM(...  4.01 us
    pallas_call x1, Pallas kernels, per_device(): pl.pallas_call(pack, out_shape=(pltpu.VMEM(edges, bf16), pltpu.VMEM(edges...  1.16 us
    pallas_call x1, Pallas kernels, per_device(): pl.pallas_call(remap, out_shape=(pltpu.HBM(shape, f32), pltpu.HBM(shape,...  1.05 us
  transfers between devices with their start and end apart: 2, of which 0 were waited for; matrix products, arithmetic and copies ran while one was open for 0% of the time, Pallas kernels for 11%

profile of v6, /device:TPU:1, one launch (start us, length us, event | category | flops | bytes accessed | tf_op | source)
XLA Modules:
  0.0 38.2 jit_solution(14790924358553317328)
XLA Ops:
  0.6 1.2 %pack.1 = (bf16[3,8,2880]{2,1,0:T(8,128)(2,1)S(1)}, bf16[3,8,2880]{2,1,0:T(8,128)(2,1)S(1)}) custom-call(bf16[4,8,2880]{2,1,0:T(8,128)(2,1)} %v_hbm.3, f32[4,8,2880]{2,1,0:T(8,128)} %thick_hbm.3, f32[4,8,2880]{2,1,0:T(8,128)} %tracer_hbm.3), custom_call_target="tpu_custom_call" | custom-call | tf_op jit(solution)/shard_map/pack/pallas_call | solution.py:600
  1.8 4.6 %collective-permute-start = (bf16[3,8,2880]{2,1,0:T(8,128)(2,1)S(1)}, bf16[3,8,2880]{2,1,0:T(8,128)(2,1)S(1)}, u32[]{:S(2)}, u32[]{:S(2)}) collective-permute-start(bf16[3,8,2880]{2,1,0:T(8,128)(2,1)S(1)} %get-tuple-element.32), channel_id=1, source_target_pairs={{8,16},{16,8},{24,32},{32,24},{40,48},{48,40},{56,64},{64,56},{72,... | collective-permute-start | bytes 414728 | tf_op jit(solution)/shard_map/ppermute | solution.py:617
  6.4 0.1 collective-permute-start.1
  6.5 4.0 %load.1 = (bf16[4,8,2880]{2,1,0:T(8,128)(2,1)S(1)}, bf16[4,8,2880]{2,1,0:T(8,128)(2,1)S(1)}, f32[4,8,2880]{2,1,0:T(8,128)S(1)}, f32[4,8,2880]{2,1,0:T(8,128)S(1)...) custom-call(s32[65]{0:T(128)} %index_hbm.1, ...), custom_call_target="tpu_custom_call" | custom-call | bytes 8392704 | tf_op jit(solution)/shard_map/load/pallas_call | solution.py:632
  10.5 0.0 collective-permute-done.next_ref
  10.5 0.0 collective-permute-done.1.near_ref
  10.5 4.3 %filter_advect.1 = (bf16[4,8,2880]{2,1,0:T(8,128)(2,1)}, bf16[4,8,2880]{2,1,0:T(8,128)(2,1)}, bf16[8,64,384]{2,1,0:T(8,128)(2,1)S(1)}, bf16[160,3072]{1,0:T(8,128)(2,1)S(1)}) custom-call(bf16[4,8,2880]{2,1,0:T(8,128)(2,1)S(1)} %get-tuple-element.24.u_ref, ...), custom_call_target="tpu_custom_call", output_to_operand_aliasing={{0}: (10, {}), {1}: (11, {}), {2}: (12, {}), {3}: (13, {})} | custom-call | tf_op jit(solution)/shard_map/filter_advect/pallas_call | solution.py:652
  14.9 22.3 %all_to_all.5.recv_ref = bf16[8,64,384]{2,1,0:T(8,128)(2,1)S(1)} all-to-all(bf16[8,64,384]{2,1,0:T(8,128)(2,1)S(1)} %get-tuple-element.41), channel_id=1, replica_groups=mesh['lat'=32,'lev'=8] {'lev'}, dimensions={0} | all-to-all | bytes 786432 | tf_op jit(solution)/shard_map/all_to_all | solution.py:672
  37.2 1.0 %remap.1 = (f32[4,64,360]{2,1,0:T(8,128)}, f32[4,64,360]{2,1,0:T(8,128)}) custom-call(f32[3,64,384]{2,1,0:T(8,128)S(1)} %get-tuple-element.40.weight_ref, bf16[8,64,384]{2,1,0:T(8,128)(2,1)S(1)} %all_to_all.5.recv_ref), custom_call_target="tpu_custom_call" | custom-call | tf_op jit(solution)/shard_map/remap/pallas_call | solution.py:674
Async XLA Ops:
  1.8 8.7 %collective-permute-start = (bf16[3,8,2880]{2,1,0:T(8,128)(2,1)S(1)}, bf16[3,8,2880]{2,1,0:T(8,128)(2,1)S(1)}, u32[]{:S(2)}, u32[]{:S(2)}) collective-permute-start(bf16[3,8,2880]{2,1,0:T(8,128)(2,1)S(1)} %get-tuple-element.32), channel_id=1, source_target_pairs={{8,16},{16,8},{24,32},{32,24},{40,48},{48,40},{56,64},{64,56},{72,... | collective-permute-start | bytes 414728 | tf_op jit(solution)/shard_map/ppermute | solution.py:617
  6.4 4.1 %collective-permute-start.1 = (bf16[3,8,2880]{2,1,0:T(8,128)(2,1)S(1)}, bf16[3,8,2880]{2,1,0:T(8,128)(2,1)S(1)}, u32[]{:S(2)}, u32[]{:S(2)}) collective-permute-start(bf16[3,8,2880]{2,1,0:T(8,128)(2,1)S(1)} %get-tuple-element.33), channel_id=1, source_target_pairs={{0,8},{8,0},{16,24},{24,16},{32,40},{40,32},{48,56},{56,48},{64,72... | collective-permute-start | bytes 414728 | tf_op jit(solution)/shard_map/ppermute | solution.py:616
